TPU v7x, 128 devices: a whole 4x4x4 slice. The times are simulated.
128 devices in a mesh: expert: 32 (over z, y, core), head: 4 (over x).
Axes of the slice: x: 4, y: 4, z: 4, core: 2. Of those that a mesh axis runs over, the one named last changes fastest.
Arguments:
- tokens: bfloat16 [16384, 1024], P('expert'), may hold values from -6 to 6
- segment_ids: int32 [32, 512], P('expert'), may hold values from 0 to 3, never falling along the last dimension, each value on 1 to 256 neighbouring positions
- expert_of: int32 [16384, 1], P('expert'), may hold values from 0 to 63; in each aligned block of 512 rows (0 to 511, 512 to 1023, ...) at most 16 rows name the same one
- norm1_gain: float32 [1024], replicated, may hold values from 0.5 to 1.5
- norm1_bias: float32 [1024], replicated, may hold values from -0.6 to 0.6
- norm2_gain: float32 [1024], replicated, may hold values from 0.5 to 1.5
- norm2_bias: float32 [1024], replicated, may hold values from -0.6 to 0.6
- w_qkv: bfloat16 [3, 1024, 1024], P(None, None, 'head'), may hold values from -0.1875 to 0.1875
- w_out: bfloat16 [1024, 1024], P('head'), may hold values from -0.75 to 0.75
- w_in: bfloat16 [64, 1024, 4096], P('expert', None, 'head'), may hold values from -0.1875 to 0.1875
- w_back: bfloat16 [64, 4096, 1024], P('expert', 'head'), may hold values from -0.09375 to 0.09375
- cotangent: float32 [16384, 1024], P('expert'), may hold values from -6 to 6
Outputs:
- output: float32 [16384, 1024], P('expert')
- grad_tokens: float32 [16384, 1024], P('expert')
- grad_norm1_gain: float32 [1024], replicated
- grad_norm1_bias: float32 [1024], replicated
- grad_norm2_gain: float32 [1024], replicated
- grad_norm2_bias: float32 [1024], replicated
- grad_w_qkv: float32 [3, 1024, 1024], P(None, None, 'head')
- grad_w_out: float32 [1024, 1024], P('head')
- grad_w_in: float32 [64, 1024, 4096], P('expert', None, 'head')
- grad_w_back: float32 [64, 4096, 1024], P('expert', 'head')
Inputs may be any that keep to these rules, and one draw needn't show every extreme that they name: `expert_of`: of the 512 tokens of one sequence, at most 16 have the same expert, and exactly 16 do for some expert in some sequence. `segment_ids`: along each sequence the segment numbers never fall; each segment covers 1 to 256 positions.
All inputs are finite; a program needn't handle non-finite values.
Results may differ from a plain program's by a relative error of at most 0.03.
Values may be sent and summed in bfloat16 or wider, within the bound.
A program may use at most 128 MiB of HBM per device.

v0:
```python
import jax
import jax.numpy as jnp
from jax import lax
from jax.sharding import PartitionSpec as P

HEAD_DIM = 64


def in_blocks(shard, dim, devices):
    before, after = (shard.shape[:dim], shard.shape[dim + 1 :])
    return jnp.moveaxis(shard.reshape(*before, devices, -1, *after), dim, 0)


def sum_at_owner(shard, axis, dim):
    blocks = in_blocks(shard, dim, lax.axis_size(axis))
    arrived = lax.all_to_all(blocks, axis, split_axis=0, concat_axis=0, tiled=True)
    return arrived.astype(jnp.float32).sum(axis=0)


def copy_for_each(shard, axis):
    devices = lax.axis_size(axis)
    return lax.all_to_all(
        jnp.broadcast_to(shard[None], (devices, *shard.shape)), axis, 0, 0, tiled=True
    )


def joined_along(blocks, dim):
    dims = list(blocks.shape[1:])
    dims[dim] *= blocks.shape[0]
    return jnp.moveaxis(blocks, 0, dim).reshape(dims)


def collect(shard, axis, dim):
    blocks = copy_for_each(shard, axis)
    return joined_along(blocks, dim)


def layer_norm(stream, gain, bias):
    center = stream - jnp.mean(stream, axis=-1, keepdims=True)
    spread = jnp.mean(center * center, axis=-1, keepdims=True)
    return center * lax.rsqrt(spread + 1e-05) * gain + bias


def activate(values):
    return jax.nn.gelu(values, approximate=True)


def slot_table(route, experts, slot_most):
    onehot = (route[:, None] == jnp.arange(experts, dtype=jnp.int32)[None, :]).astype(jnp.int32)
    earlier = jnp.cumsum(onehot, axis=0) - onehot
    rank = jnp.sum(earlier * onehot, axis=1)
    slot_index = route * slot_most + rank
    return (
        slot_index[:, None] == jnp.arange(experts * slot_most, dtype=jnp.int32)[None, :]
    ).astype(jnp.bfloat16)


def masked_scores(query, key_rows, allowed, score_scale):
    scores = (
        jnp.einsum("qhd,khd->hqk", query, key_rows, preferred_element_type=jnp.float32)
        * score_scale
    )
    return jnp.where(allowed[None], scores, -1e30)


def per_device(
    tokens,
    segment_ids,
    expert_of,
    norm1_gain,
    norm1_bias,
    norm2_gain,
    norm2_bias,
    w_qkv,
    w_out,
    w_in,
    w_back,
    cotangent,
):
    row_count, model_width = tokens.shape
    quarter = w_qkv.shape[2]
    heads_here = quarter // HEAD_DIM
    groups = lax.axis_size("expert")
    local_exp = w_in.shape[0]
    experts = local_exp * groups
    slot_most = max(2, 2 * row_count // experts)
    score_scale = HEAD_DIM ** (-0.5)
    f32 = jnp.float32
    bf16 = jnp.bfloat16
    stream = tokens.astype(f32)
    normed, norm1_back = jax.vjp(layer_norm, stream, norm1_gain, norm1_bias)
    normed_low = normed.astype(bf16)
    qkv = jnp.einsum("td,cdf->ctf", normed_low, w_qkv, preferred_element_type=f32).astype(bf16)
    query = qkv[0].reshape(row_count, heads_here, HEAD_DIM)
    key_rows = qkv[1].reshape(row_count, heads_here, HEAD_DIM)
    value_rows = qkv[2].reshape(row_count, heads_here, HEAD_DIM)
    position = jnp.arange(row_count, dtype=jnp.int32)
    segment = segment_ids[0]
    allowed = (position[:, None] >= position[None, :]) & (segment[:, None] == segment[None, :])
    scores = masked_scores(query, key_rows, allowed, score_scale)
    row_top = jnp.max(scores, axis=-1, keepdims=True)
    exponent = jnp.exp(scores - row_top)
    total = jnp.sum(exponent, axis=-1, keepdims=True)
    chances = exponent / total
    log_total = row_top + jnp.log(total)
    chances_low = chances.astype(bf16)
    mixed_heads = (
        jnp.einsum("hqk,khd->qhd", chances_low, value_rows, preferred_element_type=f32)
        .reshape(row_count, quarter)
        .astype(bf16)
    )
    attn_part = jnp.dot(mixed_heads, w_out, preferred_element_type=f32)
    attended = lax.psum(attn_part.astype(jnp.bfloat16), "head").astype(jnp.float32)
    resid = stream + attended
    normed2, norm2_back = jax.vjp(layer_norm, resid, norm2_gain, norm2_bias)
    normed2_low = normed2.astype(bf16)
    slot_onehot = slot_table(expert_of[:, 0], experts, slot_most)
    outgoing = jnp.einsum("ts,td->sd", slot_onehot, normed2_low, preferred_element_type=f32).astype(
        bf16
    )
    outgoing = outgoing.reshape(groups, local_exp, slot_most, model_width)
    received = lax.all_to_all(outgoing, "expert", split_axis=0, concat_axis=0, tiled=True)
    pre_act = jnp.einsum("nemd,edf->nemf", received, w_in, preferred_element_type=f32)
    hidden_low = activate(pre_act).astype(bf16)
    out_part = jnp.einsum("nemf,efd->nemd", hidden_low, w_back, preferred_element_type=f32)
    share_sum = sum_at_owner(out_part.astype(jnp.bfloat16), "head", 3).astype(bf16)
    returned = lax.all_to_all(share_sum, "expert", split_axis=0, concat_axis=0, tiled=True).reshape(
        experts * slot_most, quarter
    )
    expert_share = jnp.dot(slot_onehot, returned, preferred_element_type=f32).astype(bf16)
    expert_out = collect(expert_share, "head", 1).astype(f32)
    output = resid + expert_out
    cot_low = cotangent.astype(bf16)
    grad_send = jnp.einsum("ts,td->sd", slot_onehot, cot_low, preferred_element_type=f32).astype(
        bf16
    )
    grad_send = grad_send.reshape(groups, local_exp, slot_most, model_width)
    grad_recv = lax.all_to_all(grad_send, "expert", split_axis=0, concat_axis=0, tiled=True)
    pre_again = jnp.einsum("nemd,edf->nemf", received, w_in, preferred_element_type=f32)
    hidden_again, act_back = jax.vjp(activate, pre_again)
    hidden_again = hidden_again.astype(bf16)
    grad_w_back = jnp.einsum("nemf,nemd->efd", hidden_again, grad_recv, preferred_element_type=f32)
    d_hidden = jnp.einsum("nemd,efd->nemf", grad_recv, w_back, preferred_element_type=f32)
    d_pre = act_back(d_hidden)[0].astype(bf16)
    grad_w_in = jnp.einsum("nemd,nemf->edf", received, d_pre, preferred_element_type=f32)
    normed2_part = jnp.einsum("nemf,edf->nemd", d_pre, w_in, preferred_element_type=f32)
    share_grad = sum_at_owner(normed2_part.astype(jnp.bfloat16), "head", 3).astype(bf16)
    back_share = lax.all_to_all(
        share_grad, "expert", split_axis=0, concat_axis=0, tiled=True
    ).reshape(experts * slot_most, quarter)
    token_share = jnp.dot(slot_onehot, back_share, preferred_element_type=f32).astype(bf16)
    d_normed2_tok = collect(token_share, "head", 1).astype(f32)
    resid_ln, grad_gain2, grad_bias2 = norm2_back(d_normed2_tok)
    d_resid = cotangent + resid_ln
    d_att_low = d_resid.astype(bf16)
    grad_w_out = jnp.einsum("tf,td->fd", mixed_heads, d_att_low, preferred_element_type=f32)
    d_mixed = jnp.einsum("td,fd->tf", d_att_low, w_out, preferred_element_type=f32).astype(bf16)
    d_mixed = d_mixed.reshape(row_count, heads_here, HEAD_DIM)
    scores_again = masked_scores(query, key_rows, allowed, score_scale)
    chances_again = jnp.exp(scores_again - log_total)
    d_chances = jnp.einsum("qhd,khd->hqk", d_mixed, value_rows, preferred_element_type=f32)
    d_values = jnp.einsum("hqk,qhd->khd", chances_low, d_mixed, preferred_element_type=f32)
    inner = jnp.sum(chances_again * d_chances, axis=-1, keepdims=True)
    d_scores = (chances_again * (d_chances - inner)).astype(bf16)
    d_query = (
        jnp.einsum("hqk,khd->qhd", d_scores, key_rows, preferred_element_type=f32) * score_scale
    )
    d_keys = jnp.einsum("hqk,qhd->khd", d_scores, query, preferred_element_type=f32) * score_scale
    d_qkv_low = jnp.stack([d_query, d_keys, d_values]).reshape(3, row_count, quarter).astype(bf16)
    grad_w_qkv = jnp.einsum("td,ctf->cdf", normed_low, d_qkv_low, preferred_element_type=f32)
    normed_part = jnp.einsum("ctf,cdf->td", d_qkv_low, w_qkv, preferred_element_type=f32)
    d_normed = lax.psum(normed_part.astype(jnp.bfloat16), "head").astype(jnp.float32)
    stream_ln, grad_gain1, grad_bias1 = norm1_back(d_normed)
    grad_tokens = d_resid + stream_ln
    grad_w_qkv, grad_w_out, grad_gain1, grad_bias1, grad_gain2, grad_bias2 = (
        lax.psum(grad_w_qkv.astype(jnp.bfloat16), "expert").astype(jnp.float32),
        lax.psum(grad_w_out.astype(jnp.bfloat16), "expert").astype(jnp.float32),
        lax.psum(grad_gain1.astype(jnp.bfloat16), "expert").astype(jnp.float32),
        lax.psum(grad_bias1.astype(jnp.bfloat16), "expert").astype(jnp.float32),
        lax.psum(grad_gain2.astype(jnp.bfloat16), "expert").astype(jnp.float32),
        lax.psum(grad_bias2.astype(jnp.bfloat16), "expert").astype(jnp.float32),
    )
    return (
        output,
        grad_tokens,
        grad_gain1,
        grad_bias1,
        grad_gain2,
        grad_bias2,
        grad_w_qkv,
        grad_w_out,
        grad_w_in,
        grad_w_back,
    )


def solution(mesh):
    return jax.shard_map(
        per_device,
        mesh=mesh,
        in_specs=(
            P("expert", None),
            P("expert", None),
            P("expert", None),
            P(),
            P(),
            P(),
            P(),
            P(None, None, "head"),
            P("head", None),
            P("expert", None, "head"),
            P("expert", "head", None),
            P("expert", None),
        ),
        out_specs=(
            P("expert", None),
            P("expert", None),
            P(),
            P(),
            P(),
            P(),
            P(None, None, "head"),
            P("head", None),
            P("expert", None, "head"),
            P("expert", "head", None),
        ),
        check_vma=False,
    )
```

profile of v0, /device:TPU:1, one launch (start us, length us, event | category | flops | bytes accessed | tf_op | source)
XLA Modules:
  0.0 488.5 jit_solution(12560760354817886140)
XLA Ops:
  7.3 1.6 convert_reduce_fusion
  8.9 1.6 fusion.32
  21.1 2.4 reduce-window.6
  27.8 40.4 %all-reduce.6.cloned.1.call-done = bf16[512,1024]{1,0:T(8,128)(2,1)} async-done(((bf16[512,1024]{1,0:T(8,128)(2,1)}), bf16[512,1024]{1,0:T(8,128)(2,1)}) %all-reduce.6.cloned.1.call-update) | async-done | bytes 1048592 | tf_op jit(solution)/shard_map/psum | solution.py:113
  68.1 1.7 fusion.50
  70.3 3.0 fusion.40
  73.3 9.1 %all-to-all-start = ((bf16[32,2,16,1024]{3,2,1,0:T(8,128)(2,1)}), bf16[32,2,16,1024]{3,2,1,0:T(8,128)(2,1)}, u32[]{:S(2)}, u32[]{:S(2)}) async-start(bf16[32,2,16,1024]{3,2,1,0:T(8,128)(2,1)} %bitcast.173), calls=%async_computation | async-start | bytes 4194304 | tf_op jit(solution)/shard_map/all_to_all | solution.py:122
  82.4 4.3 fusion.41
  86.7 23.6 %all-to-all-done = bf16[32,2,16,1024]{3,2,1,0:T(8,128)(2,1)} async-done(((bf16[32,2,16,1024]{3,2,1,0:T(8,128)(2,1)}), bf16[32,2,16,1024]{3,2,1,0:T(8,128)(2,1)}, u32[]{:S(2)}, u32[]{:S(2)}) %all-to-all-start) | async-done | bytes 2097184 | tf_op jit(solution)/shard_map/all_to_all | solution.py:122
  110.3 7.1 %all-to-all-start.4 = ((bf16[32,2,16,1024]{3,2,1,0:T(8,128)(2,1)}), bf16[32,2,16,1024]{3,2,1,0:T(8,128)(2,1)}, u32[]{:S(2)}, u32[]{:S(2)}) async-start(bf16[32,2,16,1024]{3,2,1,0:T(8,128)(2,1)} %bitcast.172), calls=%async_computation.4 | async-start | bytes 4194304 | tf_op jit(solution)/shard_map/all_to_all | solution.py:138
  117.4 7.2 %fusion.9 = f32[2,32,16,1024]{3,2,1,0:T(8,128)} fusion(bf16[2,1024,1024]{2,1,0:T(8,128)(2,1)} %param.21, bf16[32,2,16,1024]{3,2,1,0:T(8,128)(2,1)} %all-to-all-done), kind=kOutput, calls=%fused_computation.11 | convolution fusion | flops 2147483648 | bytes 10485760 | tf_op jit(solution)/shard_map/nemd,edf->nemf/dot_general | solution.py:123
  124.6 20.6 %all-to-all-done.4 = bf16[32,2,16,1024]{3,2,1,0:T(8,128)(2,1)} async-done(((bf16[32,2,16,1024]{3,2,1,0:T(8,128)(2,1)}), bf16[32,2,16,1024]{3,2,1,0:T(8,128)(2,1)}, u32[]{:S(2)}, u32[]{:S(2)}) %all-to-all-start.4) | async-done | bytes 2097184 | tf_op jit(solution)/shard_map/all_to_all | solution.py:138
  145.2 8.7 %fusion.6 = bf16[32,2,16,1024]{3,2,0,1:T(8,128)(2,1)S(1)} fusion(f32[2,32,16,1024]{3,2,1,0:T(8,128)} %fusion.9, bf16[2,1024,1024]{2,1,0:T(8,128)(2,1)} %param.22, bf16[32,2,16,1024]{3,2,1,0:T(8,128)(2,1)} %all-to-all-done.4), kind=kOutput, calls=%fused_computation.8 | convolution fusion | flops 2168455168 | bytes 12582912 | tf_op jit(solution)/shard_map/nemd,efd->nemf/dot_general | solution.py:143
  153.9 2.4 fusion.45
  157.8 4.5 all-to-all-start.5
  162.3 6.1 %fusion.42 = bf16[2,32,16,1024]{3,2,1,0:T(8,128)(2,1)S(1)} fusion(bf16[2,1024,1024]{2,1,0:T(8,128)(2,1)} %param.22, f32[2,32,16,1024]{3,2,1,0:T(8,128)} %fusion.9), kind=kOutput, calls=%fused_computation.72 | convolution fusion | flops 2157969408 | bytes 10485760 | tf_op jit(solution)/shard_map/nemf,efd->nemd/dot_general | solution.py:125
  169.9 16.4 %all-to-all-done.5 = bf16[4,32,2,16,256]{4,3,1,2,0:T(8,128)(2,1)} async-done(((bf16[4,32,2,16,256]{4,3,1,2,0:T(8,128)(2,1)}), bf16[4,32,2,16,256]{4,3,1,2,0:T(8,128)(2,1)}, u32[]{:S(2)}, u32[]{:S(2)}) %all-to-all-start.5) | async-done | bytes 2097184 | tf_op jit(solution)/shard_map/all_to_all | solution.py:16
  186.4 4.5 all-to-all-start.1
  190.8 2.9 reduce_sum.207
  193.7 1.9 copy.110
  195.6 18.4 %all-to-all-done.1 = bf16[4,32,2,16,256]{4,3,1,2,0:T(8,128)(2,1)} async-done(((bf16[4,32,2,16,256]{4,3,1,2,0:T(8,128)(2,1)}), bf16[4,32,2,16,256]{4,3,1,2,0:T(8,128)(2,1)}, u32[]{:S(2)}, u32[]{:S(2)}) %all-to-all-start.1) | async-done | bytes 2097184 | tf_op jit(solution)/shard_map/all_to_all | solution.py:16
  213.9 12.4 %all-to-all-start.6 = ((bf16[32,2,16,256]{3,2,1,0:T(8,128)(2,1)}), bf16[32,2,16,256]{3,2,1,0:T(8,128)(2,1)}, u32[]{:S(2)}, u32[]{:S(2)}) async-start(bf16[32,2,16,256]{3,2,1,0:T(8,128)(2,1)} %copy.110), calls=%async_computation.6 | async-start | bytes 1048576 | tf_op jit(solution)/shard_map/all_to_all | solution.py:148
  226.3 2.9 reduce_sum.206
  229.2 1.9 copy.105
  231.1 6.7 %all-to-all-done.6 = bf16[32,2,16,256]{3,2,1,0:T(8,128)(2,1)} async-done(((bf16[32,2,16,256]{3,2,1,0:T(8,128)(2,1)}), bf16[32,2,16,256]{3,2,1,0:T(8,128)(2,1)}, u32[]{:S(2)}, u32[]{:S(2)}) %all-to-all-start.6) | async-done | bytes 524320 | tf_op jit(solution)/shard_map/all_to_all | solution.py:148
  237.8 4.7 all-to-all-start.2
  242.4 2.3 fusion.57
  244.7 9.4 %all-to-all-done.2 = bf16[32,2,16,256]{3,2,1,0:T(8,128)(2,1)} async-done(((bf16[32,2,16,256]{3,2,1,0:T(8,128)(2,1)}), bf16[32,2,16,256]{3,2,1,0:T(8,128)(2,1)}, u32[]{:S(2)}, u32[]{:S(2)}) %all-to-all-start.2) | async-done | bytes 524320 | tf_op jit(solution)/shard_map/all_to_all | solution.py:127
  254.1 2.0 broadcast_in_dim.31
  256.1 4.3 all-to-all-start.7
  260.4 9.0 %convolution_bitcast_fusion = f32[2,1024,1024]{2,1,0:T(8,128)} fusion(bf16[32,2,16,1024]{3,2,1,0:T(8,128)(2,1)} %all-to-all-done.4, f32[2,32,16,1024]{3,2,1,0:T(8,128)} %fusion.9), kind=kOutput, calls=%fused_computation.31 | convolution fusion | flops 2156920832 | bytes 14680064 | tf_op jit(solution)/shard_map/nemf,nemd->efd/dot_general | solution.py:142
  269.4 2.3 fusion.56
  271.6 3.6 all-to-all-done.7
  275.2 2.0 broadcast_in_dim.30
  277.2 4.3 all-to-all-start.3
  285.2 10.2 %all-to-all-done.3 = bf16[4,512,256]{2,1,0:T(8,128)(2,1)} async-done(((bf16[4,512,256]{2,1,0:T(8,128)(2,1)}), bf16[4,512,256]{2,1,0:T(8,128)(2,1)}, u32[]{:S(2)}, u32[]{:S(2)}) %all-to-all-start.3) | async-done | bytes 1048608 | tf_op jit(solution)/shard_map/all_to_all | solution.py:22
  298.7 2.3 fusion.85
  305.2 1.5 multiply_reduce_fusion
  312.7 2.9 bitcast_convert_fusion
  316.0 8.1 %convolution_bitcast_fusion.1 = f32[2,1024,1024]{2,1,0:T(8,128)} fusion(bf16[32,2,16,1024]{3,2,1,0:T(8,128)(2,1)} %all-to-all-done, bf16[32,2,16,1024]{3,2,0,1:T(8,128)(2,1)} %copy-done.41), kind=kOutput, calls=%fused_computation.32 | convolution fusion | flops 2147483648 | bytes 12582912 | tf_op jit(solution)/shard_map/nemd,nemf->edf/dot_general | solution.py:145
  325.5 2.4 fusion.53
  329.3 29.0 %all-reduce.8.cloned.1.call-done = bf16[512,1024]{1,0:T(8,128)(2,1)} async-done(((bf16[512,1024]{1,0:T(8,128)(2,1)}), bf16[512,1024]{1,0:T(8,128)(2,1)}) %all-reduce.8.cloned.1.call-update) | async-done | bytes 1048592 | tf_op jit(solution)/shard_map/psum | solution.py:172
  359.8 1.8 fusion.33
  362.9 65.5 %all-reduce = (bf16[1024]{0:T(1024)(128)(2,1)S(1)}, bf16[1024]{0:T(1024)(128)(2,1)S(1)}, bf16[1024]{0:T(1024)(128)(2,1)S(1)}, bf16[1024]{0:T(1024)(128)(2,1)S(1)}) all-reduce(bf16[1024]{0:T(1024)(128)(2,1)S(1)} %get-tuple-element.62, bf16[1024]{0:T(1024)(128)(2,1)S(1)} %reduce_sum.214, ...), channel_id=1, replica_groups=mesh['expert'=32,'head'=4] {'expert'}, use_global_device_ids=true, to_apply=%region_19.20 | all-reduce | flops 4096 | bytes 16384 | tf_op jit(solution)/shard_map/psum | solution.py:178
  430.8 41.6 %all-reduce.10.cloned.1.call-done = (bf16[3,1024,256]{1,2,0:T(8,128)(2,1)}, bf16[256,1024]{1,0:T(8,128)(2,1)}) async-done(((bf16[3,1024,256]{1,2,0:T(8,128)(2,1)}, bf16[256,1024]{1,0:T(8,128)(2,1)}), (bf16[3,1024,256]{1,2,0:T(8,128)(2,1)}, bf16[256,1024]{1,0:T(8,128)(2,1)})) %all-reduce.10.cloned.1.call-update) | async-done | bytes 2097168 | tf_op jit(solution)/shard_map/psum | solution.py:176
  472.4 2.1 convert_element_type.194
  474.5 3.1 copy.121
  477.6 3.9 add_add_fusion.2
  (139 shorter events, 43.4 us)
Async XLA Ops:
  7.2 4.1 copy-start
  7.2 4.1 copy-start.3
  7.2 3.9 copy-start.36
  7.2 4.1 copy-start.28
  7.2 4.1 copy-start.39
  7.2 60.9 %all-reduce.6.cloned.1.call-start = ((), (), s32[]{:S(2)}) async-start(), calls=%async_computation.8 | async-start | bytes 2097152 | tf_op jit(solution)/shard_map/psum | solution.py:113
  8.9 3.7 copy-start.26
  11.1 1.5 copy-start.31
  12.6 3.8 copy-start.14
  13.6 1.9 copy-start.1
  16.4 1.3 copy-start.6
  16.5 2.5 copy-start.19
  18.2 2.2 copy-start.30
  27.8 42.5 %copy-start.35 = (f32[1024]{0:T(1024)S(1)}, f32[1024]{0:T(1024)}, u32[]{:S(2)}) copy-start(f32[1024]{0:T(1024)} %param.17) | copy-start | bytes 12292
  27.8 42.5 %copy-start.38 = (f32[1024]{0:T(1024)S(1)}, f32[1024]{0:T(1024)}, u32[]{:S(2)}) copy-start(f32[1024]{0:T(1024)} %param.18) | copy-start | bytes 12292
  68.1 1.7 copy-start.11
  73.3 37.0 %all-to-all-start = ((bf16[32,2,16,1024]{3,2,1,0:T(8,128)(2,1)}), bf16[32,2,16,1024]{3,2,1,0:T(8,128)(2,1)}, u32[]{:S(2)}, u32[]{:S(2)}) async-start(bf16[32,2,16,1024]{3,2,1,0:T(8,128)(2,1)} %bitcast.173), calls=%async_computation | async-start | bytes 4194304 | tf_op jit(solution)/shard_map/all_to_all | solution.py:122
  110.3 34.9 %all-to-all-start.4 = ((bf16[32,2,16,1024]{3,2,1,0:T(8,128)(2,1)}), bf16[32,2,16,1024]{3,2,1,0:T(8,128)(2,1)}, u32[]{:S(2)}, u32[]{:S(2)}) async-start(bf16[32,2,16,1024]{3,2,1,0:T(8,128)(2,1)} %bitcast.172), calls=%async_computation.4 | async-start | bytes 4194304 | tf_op jit(solution)/shard_map/all_to_all | solution.py:138
  145.2 8.7 %copy-start.37 = (bf16[2,1024,1024]{2,1,0:T(8,128)(2,1)S(1)}, bf16[2,1024,1024]{2,1,0:T(8,128)(2,1)}, u32[]{:S(2)}) copy-start(bf16[2,1024,1024]{2,1,0:T(8,128)(2,1)} %param.21) | copy-start | bytes 12582916
  153.9 2.4 copy-start.41
  157.8 28.5 %all-to-all-start.5 = ((bf16[4,32,2,16,256]{4,3,1,2,0:T(8,128)(2,1)}), bf16[4,32,2,16,256]{4,3,1,2,0:T(8,128)(2,1)}, u32[]{:S(2)}, u32[]{:S(2)}) async-start(bf16[4,32,2,16,256]{4,3,1,2,0:T(8,128)(2,1)} %bitcast.160), calls=%async_computation.5 | async-start | bytes 4194304 | tf_op jit(solution)/shard_map/all_to_all | solution.py:16
  186.4 27.6 %all-to-all-start.1 = ((bf16[4,32,2,16,256]{4,3,1,2,0:T(8,128)(2,1)}), bf16[4,32,2,16,256]{4,3,1,2,0:T(8,128)(2,1)}, u32[]{:S(2)}, u32[]{:S(2)}) async-start(bf16[4,32,2,16,256]{4,3,1,2,0:T(8,128)(2,1)} %bitcast.159), calls=%async_computation.1 | async-start | bytes 4194304 | tf_op jit(solution)/shard_map/all_to_all | solution.py:16
  213.9 23.8 %all-to-all-start.6 = ((bf16[32,2,16,256]{3,2,1,0:T(8,128)(2,1)}), bf16[32,2,16,256]{3,2,1,0:T(8,128)(2,1)}, u32[]{:S(2)}, u32[]{:S(2)}) async-start(bf16[32,2,16,256]{3,2,1,0:T(8,128)(2,1)} %copy.110), calls=%async_computation.6 | async-start | bytes 1048576 | tf_op jit(solution)/shard_map/all_to_all | solution.py:148
  237.8 16.4 %all-to-all-start.2 = ((bf16[32,2,16,256]{3,2,1,0:T(8,128)(2,1)}), bf16[32,2,16,256]{3,2,1,0:T(8,128)(2,1)}, u32[]{:S(2)}, u32[]{:S(2)}) async-start(bf16[32,2,16,256]{3,2,1,0:T(8,128)(2,1)} %copy.105), calls=%async_computation.2 | async-start | bytes 1048576 | tf_op jit(solution)/shard_map/all_to_all | solution.py:127
  256.1 19.1 %all-to-all-start.7 = ((bf16[4,512,256]{2,1,0:T(8,128)(2,1)}), bf16[4,512,256]{2,1,0:T(8,128)(2,1)}, u32[]{:S(2)}, u32[]{:S(2)}) async-start(bf16[4,512,256]{2,1,0:T(8,128)(2,1)} %broadcast_in_dim.31), calls=%async_computation.7 | async-start | bytes 2097152 | tf_op jit(solution)/shard_map/all_to_all | solution.py:22
  277.2 18.2 %all-to-all-start.3 = ((bf16[4,512,256]{2,1,0:T(8,128)(2,1)}), bf16[4,512,256]{2,1,0:T(8,128)(2,1)}, u32[]{:S(2)}, u32[]{:S(2)}) async-start(bf16[4,512,256]{2,1,0:T(8,128)(2,1)} %broadcast_in_dim.30), calls=%async_computation.3 | async-start | bytes 2097152 | tf_op jit(solution)/shard_map/all_to_all | solution.py:22
  281.5 76.9 %all-reduce.8.cloned.1.call-start = ((), (), s32[]{:S(2)}) async-start(), calls=%async_computation.9 | async-start | bytes 2097152 | tf_op jit(solution)/shard_map/psum | solution.py:172
  283.2 2.0 copy-start.8
  296.8 1.6 copy-start.9
  296.8 1.8 copy-start.13
  298.7 2.3 copy-start.18
  300.9 1.8 copy-start.7
  302.0 2.2 copy-start.4
  302.0 3.2 copy-start.2
  302.0 3.2 copy-start.15
  308.0 2.7 copy-start.21
  309.5 2.4 copy-start.22
  311.9 3.8 copy-start.23
  315.7 8.5 %copy-start.17 = (bf16[4,64,512]{2,1,0:T(8,128)(2,1)S(1)}, bf16[4,64,512]{2,1,0:T(8,128)(2,1)}, u32[]{:S(2)}) copy-start(bf16[4,64,512]{2,1,0:T(8,128)(2,1)} %copy-done.16) | copy-start | bytes 786436
  315.7 156.7 %all-reduce.10.cloned.1.call-start = ((), (), s32[]{:S(2)}) async-start(), calls=%async_computation.10 | async-start | bytes 4194304 | tf_op jit(solution)/shard_map/psum | solution.py:176
  316.0 8.2 %copy-start.5 = (f32[512,1024]{1,0:T(8,128)S(1)}, f32[512,1024]{1,0:T(8,128)}, u32[]{:S(2)}) copy-start(f32[512,1024]{1,0:T(8,128)} %copy-done.4) | copy-start | bytes 6291460
  324.2 1.3 copy-start.24
  324.2 1.3 copy-start.25
  324.2 1.3 copy-start.27
  324.2 1.3 copy-start.29
  324.2 1.3 copy-start.32
  327.9 33.7 %copy-start.34 = (f32[512]{0:T(512)S(1)}, f32[512]{0:T(512)}, u32[]{:S(2)}) copy-start(f32[512]{0:T(512)} %copy-done.33) | copy-start | bytes 6148
  359.8 1.9 copy-start.10
  (5 other events, 4.9 us)
Sparse Core Ops, SparseCore 0:
  20.5 47.5 all-reduce.5
  315.8 42.5 all-reduce.7
  362.3 110.0 all-reduce.9
where the time goes:
time: 498 us; the launch traced here: 488 us
  waiting for transfers between devices  220 us (44%)
  matrix products  69.9 us (14%)
  blocking collectives  65.5 us (13%)
  starting transfers between devices  51.1 us (10%)
  other arithmetic  40.9 us (8%)
  local copies, waits for them, and re-layouts  26.3 us (5%)
  between operations  14.8 us (3%)
    psum x1, blocking collectives, per_device(): lax.psum(grad_gain1.astype(jnp.bfloat16), 'expert').astype(jnp.float32)  65.5 us
    psum x1, waiting for transfers between devices, per_device(): lax.psum(grad_w_qkv.astype(jnp.bfloat16), 'expert').astype(jnp.float32)  41.6 us
    psum x1, waiting for transfers between devices, per_device(): lax.psum(attn_part.astype(jnp.bfloat16), 'head').astype(jnp.float32)  40.4 us
    all_to_all x2, waiting for transfers between devices, sum_at_owner(): lax.all_to_all(blocks, axis, split_axis=0, concat_axis=0, tiled=True)  34.8 us
    psum x1, waiting for transfers between devices, per_device(): lax.psum(normed_part.astype(jnp.bfloat16), 'head').astype(jnp.float32)  29 us
    all_to_all x1, waiting for transfers between devices, per_device(): lax.all_to_all(outgoing, 'expert', split_axis=0, concat_axis=0, tiled=True)  23.6 us
    all_to_all x1, waiting for transfers between devices, per_device(): lax.all_to_all(grad_send, 'expert', split_axis=0, concat_axis=0, tiled=True)  20.6 us
    all_to_all x2, waiting for transfers between devices, copy_for_each(): lax.all_to_all(jnp.broadcast_to(shard[None], (devices, *shard.shape)), ax...  13.8 us
  transfers between devices with their start and end apart: 11, of which 11 were waited for; matrix products, arithmetic and copies ran while one was open for 15% of the time, Pallas kernels for 0%

commit v1 on v0

v1 whole, which is shorter than its diff:
```python
import functools

import jax
import jax.numpy as jnp
from jax import lax
from jax.experimental import pallas as pl
from jax.experimental.pallas import tpu as pltpu
from jax.sharding import PartitionSpec as P

f32 = jnp.float32
bf16 = jnp.bfloat16
i32 = jnp.int32
MESH = pl.DeviceIdType.MESH

T = 512
D = 1024
G = 32
H = 4
Q = T // H
HALF = D // 2
EPS = 1e-5


def mm(a, b):
    return lax.dot_general(a, b, (((1,), (0,)), ((), ())), preferred_element_type=f32)


def mm_nt(a, b):
    return lax.dot_general(a, b, (((1,), (1,)), ((), ())), preferred_element_type=f32)


def iota(shape, dim):
    return lax.broadcasted_iota(i32, shape, dim)


def hot(cond):
    return jnp.where(cond, 1.0, 0.0).astype(bf16)


def rem4(v):
    return lax.rem(v, 4)


def remote(src, dst, send_sem, recv_sem, device):
    return pltpu.make_async_remote_copy(
        src_ref=src,
        dst_ref=dst,
        send_sem=send_sem,
        recv_sem=recv_sem,
        device_id=device,
        device_id_type=MESH,
    )


def columns(ref, rows):
    half = ref.shape[1] // 2
    return lambda b, hf: ref.at[pl.ds(pl.multiple_of(b * rows, rows), rows), pl.ds(hf * half, half)]


class ReduceScatter:
    def __init__(self, ring, part, relay, total, arrived, send, recv):
        self.me, right, left = ring
        self.right, self.left = rem4(self.me + 1), rem4(self.me + 3)
        far = rem4(self.me + 2)
        self.part, self.relay, self.total, self.arrived = part, relay, total, arrived
        self.far = [
            remote(part(far, 0), relay(0), send.at[0], recv.at[0], left),
            remote(part(far, 1), relay(1), send.at[1], recv.at[1], right),
        ]
        self.near = [
            remote(part(self.left, 1), arrived(1, 1), send.at[2], recv.at[2], left),
            remote(part(self.right, 0), arrived(0, 0), send.at[3], recv.at[3], right),
        ]
        self.last = [
            remote(total(0), arrived(1, 0), send.at[4], recv.at[4], left),
            remote(total(1), arrived(0, 1), send.at[5], recv.at[5], right),
        ]

    def send_far(self, hf):
        self.far[hf].start()

    def send_near(self, side):
        self.near[side].start()

    def pass_on(self):
        for hf, owner in ((0, self.left), (1, self.right)):
            self.far[hf].wait_recv()
            mine = self.part(owner, hf)[...].astype(f32)
            self.total(hf)[...] = (mine + self.relay(hf)[...].astype(f32)).astype(bf16)
            self.last[hf].start()

    def wait(self):
        for copy in self.near + self.last:
            copy.wait_recv()

    def value(self, hf):
        mine = self.part(self.me, hf)[...].astype(f32)
        return mine + self.arrived(0, hf)[...].astype(f32) + self.arrived(1, hf)[...].astype(f32)

    def wait_sent(self):
        for copy in self.far + self.near + self.last:
            copy.wait_send()


class Gather:
    def __init__(self, ring, block, send, recv):
        me, right, left = ring
        on_right, on_left = rem4(me + 1), rem4(me + 3)

        def copy(b, hf, i, device):
            return remote(block(b, hf), block(b, hf), send.at[i], recv.at[i], device)

        self.first = [copy(me, 0, 0, right), copy(me, 1, 1, left)]
        self.second = [copy(me, 0, 2, left), copy(me, 1, 3, right)]
        self.third = [copy(on_left, 0, 4, right), copy(on_right, 1, 5, left)]

    def start(self):
        for copy in self.first + self.second:
            copy.start()

    def pass_on(self, hf):
        self.first[hf].wait_recv()
        self.third[hf].start()

    def wait_second(self, hf):
        self.second[hf].wait_recv()

    def wait_third(self, hf):
        self.third[hf].wait_recv()

    def finish(self):
        self.pass_on(0)
        self.pass_on(1)
        for copy in self.second + self.third:
            copy.wait_recv()

    def wait_sent(self):
        for copy in self.first + self.second + self.third:
            copy.wait_send()


def norm_parts(x):
    center = x - jnp.mean(x, axis=-1, keepdims=True)
    r = lax.rsqrt(jnp.mean(center * center, axis=-1, keepdims=True) + EPS)
    return center * r, r


def norm_back(g, xhat, r):
    return r * (
        g - jnp.mean(g, axis=-1, keepdims=True) - xhat * jnp.mean(g * xhat, axis=-1, keepdims=True)
    )


def gelu_parts(v):
    c = 0.7978845608028654
    v2 = v * v
    t = jnp.tanh(c * v * (1.0 + 0.044715 * v2))
    half = 0.5 * (1.0 + t)
    grad = half + 0.5 * v * (1.0 - t * t) * c * (1.0 + 3.0 * 0.044715 * v2)
    return v * half, grad


def as_tile(row):
    return jnp.concatenate([row[:, i * 128 : (i + 1) * 128] for i in range(8)], axis=0)


def layer_kernel(
    seg_ref, route_ref, g1_ref, b1_ref, g2_ref, b2_ref,
    tok_hbm, wqkv_hbm, wout_hbm, win_hbm, wbk_hbm, cot_hbm,
    x_out, g_out, hid_out, dpre_out, u_out, gt_out, w_out, nrm_out,
    tok, wqkv, wout, win, wbk, cotw, cot_low,
    pm, pmt, code_c, code_r, slot_c, slot_r,
    csend, crecv, gal,
    xp, normed, normed_t, qkv, q_t, chs, mixed, mixed_t,
    apart, a_rel, a_sum, a_arr,
    nsend, nrecv, xall, hid, dpre, n2p,
    e_rel, e_sum, e_arr, esend, erecv,
    o_rel, o_sum, o_arr, osend, orecv, outall,
    datt, dmx, dm_t, dqkv,
    d_rel, d_sum, d_arr, gtall,
    wpart, wx, ws,
    w0, w0_rel, w0_sum, w0_arr, w1, w1_rel, w1_sum, w1_arr,
    w2_rel, w2_sum, w2_arr, w3_rel, w3_sum, w3_arr,
    nv, nrx, nye,
    loc, cs, cr, ns, nr, es, er, os_, or_, rss, rsr, ags, agr, xs, xr, vs, vr, vys, vyr,
):
    me = lax.axis_index("expert")
    h = lax.axis_index("head")
    core = lax.rem(me, 2)
    chip = me // 2
    y = lax.rem(chip, 4)
    z = chip // 4

    def at_yz(yy, zz, cc):
        return {"expert": (rem4(zz) * 4 + rem4(yy)) * 2 + cc}

    ring_x = (h, {"head": rem4(h + 1)}, {"head": rem4(h + 3)})
    ring_y = (y, at_yz(y + 1, z, core), at_yz(y + 3, z, core))
    ring_z = (z, at_yz(y, z + 1, core), at_yz(y, z + 3, core))
    sibling = {"expert": chip * 2 + 1 - core}
    left, right, far = rem4(h + 3), rem4(h + 1), rem4(h + 2)

    att_q, dres = cotw.at[pl.ds(0, Q), :], cotw.at[pl.ds(Q, Q), :]
    npart = tok
    dss = [tok.at[:, pl.ds(0, T)], tok.at[:, pl.ds(T, T)]]

    def outp(q, e):
        return csend.at[e, pl.ds(pl.multiple_of(q * Q, Q), Q), :]

    loads = {}
    for i, (name, src, dst) in enumerate(
        (
            ("cot", cot_hbm, cotw),
            ("tok", tok_hbm, tok),
            ("wqkv", wqkv_hbm, wqkv),
            ("wout", wout_hbm, wout),
            ("win", win_hbm, win),
            ("wbk", wbk_hbm, wbk),
        )
    ):
        loads[name] = pltpu.make_async_copy(src, dst, loc.at[i])
        loads[name].start()

    barrier = pltpu.get_barrier_semaphore()

    @pl.loop(1, G)
    def _(k):
        pl.semaphore_signal(
            barrier, inc=1, device_id={"expert": lax.rem(me + k, G)}, device_id_type=MESH
        )

    for k in range(1, H):
        pl.semaphore_signal(barrier, inc=1, device_id={"head": rem4(h + k)}, device_id_type=MESH)

    route_c = route_ref[...]
    eye = iota((T, T), 0) == iota((T, T), 1)

    def to_row(col):
        return jnp.sum(jnp.where(eye, col.astype(f32), 0.0), axis=0, keepdims=True)

    onehot = jnp.where(iota((T, 128), 1) == route_c, 1.0, 0.0)
    before = hot(iota((T, T), 1) < iota((T, T), 0))
    rank = jnp.sum(mm(before, onehot.astype(bf16)) * onehot, axis=1, keepdims=True)
    count = jnp.broadcast_to(jnp.sum(onehot, axis=0, keepdims=True), (8, 128)).astype(bf16)
    first = mm(count, hot(iota((128, 128), 0) < iota((128, 128), 1)))[0:1]
    place = (jnp.sum(onehot * first, axis=1, keepdims=True) + rank).astype(i32)
    rank4 = rank.astype(i32) >> 2
    quarter = place & 3
    pos_c = quarter * Q + (place >> 2)
    slot4 = route_c * 4 + rank4
    key = (route_c & 1) * T + (route_c >> 1) * 16 + quarter * 4 + rank4
    pos_r = to_row(pos_c).astype(i32)
    key_r = to_row(key).astype(i32)
    perm = iota((T, T), 0) == pos_r
    perm_t = iota((T, T), 1) == pos_c
    pm[...] = hot(perm)
    pmt[...] = hot(perm_t)
    code = (seg_ref[...] * 1024 + iota((1, T), 1)).astype(f32)
    code_pc = jnp.sum(jnp.where(perm, code, 0.0), axis=1, keepdims=True)
    code_c[...] = code_pc.astype(i32)
    code_r[...] = to_row(code_pc).astype(i32)
    own_t = iota((T, Q), 1) + h * Q == pos_c
    slot_row = jnp.sum(jnp.where(own_t, slot4.astype(f32), 0.0), axis=0, keepdims=True)
    slot_r[...] = slot_row.astype(i32)
    eye_q = iota((Q, Q), 0) == iota((Q, Q), 1)
    slot_c[...] = jnp.sum(jnp.where(eye_q, slot_row, 0.0), axis=1, keepdims=True).astype(i32)

    pl.semaphore_wait(barrier, G - 1 + H - 1)

    loads["cot"].wait()
    cot_low[...] = cotw[...].astype(bf16)

    def cot_copy(d):
        return remote(
            csend.at[:, pl.ds(pl.multiple_of(d * 16, 16), 16), :],
            crecv.at[:, pl.ds(pl.multiple_of(me * 16, 16), 16), :],
            cs.at[d], cr.at[me], {"expert": d},
        )

    def cot_arrived(d):
        return remote(
            csend.at[:, pl.ds(pl.multiple_of(d * 16, 16), 16), :],
            crecv.at[:, pl.ds(pl.multiple_of(d * 16, 16), 16), :],
            cs.at[d], cr.at[d], {"expert": d},
        )

    def row_copy(src, dst, send, recv):
        def to(d):
            return remote(
                src.at[pl.ds(pl.multiple_of(d * 16, 16), 16), :],
                dst.at[pl.ds(pl.multiple_of(me * 16, 16), 16), :],
                send.at[d], recv.at[me], {"expert": d},
            )

        def arrived(d):
            return remote(
                src.at[pl.ds(pl.multiple_of(d * 16, 16), 16), :],
                dst.at[pl.ds(pl.multiple_of(d * 16, 16), 16), :],
                send.at[d], recv.at[d], {"expert": d},
            )

        return to, arrived

    def start_chunk(to, chunk):
        @pl.loop(0, 8)
        def _(k):
            d = chunk * 8 + lax.rem(me + k, 8)

            @pl.when(d != me)
            def _():
                to(d).start()

    def others(act):
        @pl.loop(1, G)
        def _(k):
            act(lax.rem(me + k, G))

    @pl.loop(0, 4)
    def _(c):
        chunk = rem4(me // 8 + c)
        row0 = pl.multiple_of(chunk * 128, 128)
        for e in range(2):
            sel = hot(iota((128, T), 0) + (row0 + e * T) == key_r)
            csend[e, pl.ds(row0, 128), :] = mm(sel, cot_low[...]).astype(bf16)
        start_chunk(cot_copy, chunk)

    own16 = pl.ds(pl.multiple_of(me * 16, 16), 16)
    crecv[:, own16, :] = csend[:, own16, :]

    loads["tok"].wait()

    @pl.loop(0, 4)
    def _(rb):
        rows = pl.ds(pl.multiple_of(rb * Q, Q), Q)
        x = mm(pm[rows, :], tok[...])
        xp[rows, :] = x.astype(bf16)
        xhat, _r = norm_parts(x)
        normed[rows, :] = (xhat * g1_ref[...] + b1_ref[...]).astype(bf16)

    loads["wqkv"].wait()

    @pl.loop(0, 3)
    def _(c):
        qkv[c] = mm(normed[...], wqkv[c]).astype(bf16)

    for hp in range(2):
        pair = slice(hp * 128, hp * 128 + 128)

        @pl.loop(0, 4)
        def _(rb):
            rows = pl.ds(pl.multiple_of(rb * Q, Q), Q)
            codes = code_c[rows, :]
            keys = code_r[...]
            allowed = (keys <= codes) & (keys >= ((codes >> 10) << 10))
            outs = []
            for hh in range(2):
                lanes = slice(hp * 128 + hh * 64, hp * 128 + hh * 64 + 64)
                s = mm_nt(qkv[0, rows, lanes], qkv[1, :, lanes]) * 0.125
                s = jnp.where(allowed, s, -1e30)
                e = jnp.exp(s - jnp.max(s, axis=-1, keepdims=True))
                ch = (e * (1.0 / jnp.sum(e, axis=-1, keepdims=True))).astype(bf16)
                chs[hp * 2 + hh, rows, :] = ch
                outs.append(mm(ch, qkv[2, :, lanes]))
            mixed[rows, pair] = jnp.concatenate(outs, axis=1).astype(bf16)

    loads["wout"].wait()
    halves = lambda ref: (lambda hf: ref.at[hf])
    sides = lambda ref: (lambda side, hf: ref.at[side, hf])
    rs_a = ReduceScatter(
        ring_x, columns(apart, Q), halves(a_rel), halves(a_sum), sides(a_arr), rss.at[0], rsr.at[0]
    )

    def project(b):
        rows = pl.ds(pl.multiple_of(b * Q, Q), Q)
        apart[rows, :] = mm(mixed[rows, :], wout[...]).astype(bf16)

    project(far)
    rs_a.send_far(0)
    rs_a.send_far(1)
    project(left)
    rs_a.send_near(0)
    project(right)
    rs_a.send_near(1)
    project(h)
    own_rows = pl.ds(pl.multiple_of(h * Q, Q), Q)

    rs_a.pass_on()
    q_t[...] = qkv[0].astype(f32).T.astype(bf16)
    mixed_t[...] = mixed[...].astype(f32).T.astype(bf16)

    @pl.loop(0, 4)
    def _(c):
        cols = pl.ds(pl.multiple_of(c * 256, 256), 256)
        normed_t[cols, :] = normed[:, cols].astype(f32).T.astype(bf16)

    rs_a.wait()
    att_q[...] = jnp.concatenate([rs_a.value(0), rs_a.value(1)], axis=1)

    def resid_norm():
        return norm_parts(xp[own_rows, :].astype(f32) + att_q[...])

    xhat2, _r2 = resid_norm()
    normed2 = (xhat2 * g2_ref[...] + b2_ref[...]).astype(bf16)
    n_to, n_arrived = row_copy(nsend, nrecv, ns, nr)

    def pick_halves(full, row0):
        low_half = ((iota((128, HALF), 0) + row0) & 8) == 0
        return jnp.where(low_half, full[:, :HALF], full[:, HALF:]).astype(bf16)

    for c in range(4):
        chunk = rem4(me // 8 + c)
        row0 = pl.multiple_of(chunk * 128, 128)
        r = iota((128, Q), 0) + row0
        sel = hot((r >> 4) * 8 + (r & 7) == slot_r[...])
        nsend[pl.ds(row0, 128), :] = pick_halves(mm(sel, normed2), row0)
        start_chunk(n_to, chunk)
    nrecv[own16, :] = nsend[own16, :]

    others(lambda d: cot_arrived(d).wait_recv())

    @pl.loop(0, 4)
    def _(q):
        i = iota((128, T), 0)
        sel = hot((i >> 2) * 16 + (i & 3) + q * 4 == iota((128, T), 1))
        for e in range(2):
            gal[q, e] = mm(sel, crecv[e]).astype(bf16)

    others(lambda d: n_arrived(d).wait_recv())
    ag_x = Gather(ring_x, lambda b, hf: xall.at[b, hf], ags.at[0], agr.at[0])
    for e in range(2):
        i = iota((128, T), 0)
        target = (i >> 2) * 16 + e * 4 + (i & 3)
        for hf in range(2):
            sel = hot(iota((128, T), 1) == target + hf * 8)
            xall[h, e, :, hf * HALF : (hf + 1) * HALF] = mm(sel, nrecv[...]).astype(bf16)
    ag_x.start()

    loads["win"].wait()
    loads["wbk"].wait()
    others(lambda d: cot_copy(d).wait_send())

    def unit(q, e):
        @pl.loop(0, 4)
        def _(c):
            cols = pl.ds(pl.multiple_of(c * 256, 256), 256)
            act, slope = gelu_parts(mm(xall[q, e], win[e, :, cols]))
            hid[q, e, :, cols] = act.astype(bf16)
            dpre[q, e, :, cols] = (mm_nt(gal[q, e], wbk[e, cols, :]) * slope).astype(bf16)

    def unit_n2(q, e):
        @pl.loop(0, 4)
        def _(c):
            cols = pl.ds(pl.multiple_of(c * 256, 256), 256)
            n2p[q, e, :, cols] = mm_nt(dpre[q, e], win[e, cols, :]).astype(bf16)

    def unit_out(q, e):
        @pl.loop(0, 4)
        def _(c):
            cols = pl.ds(pl.multiple_of(c * 256, 256), 256)
            outp(q, e)[:, cols] = mm(hid[q, e], wbk[e, :, cols]).astype(bf16)

    rs_e = ReduceScatter(
        ring_x, lambda b, hf: n2p.at[b, hf], halves(e_rel), halves(e_sum), sides(e_arr),
        rss.at[1], rsr.at[1],
    )
    rs_o = ReduceScatter(
        ring_x, outp, halves(o_rel), halves(o_sum), sides(o_arr),
        rss.at[2], rsr.at[2],
    )

    def whole(q, e):
        unit(q, e)
        unit_n2(q, e)
        unit_out(q, e)

    whole(h, 0)
    whole(h, 1)
    ag_x.pass_on(0)
    ag_x.pass_on(1)
    whole(left, 0)
    whole(right, 1)
    ag_x.wait_second(0)
    whole(right, 0)
    rs_e.send_near(1)
    ag_x.wait_second(1)
    whole(left, 1)
    rs_e.send_near(0)
    ag_x.wait_third(0)
    unit(far, 0)
    unit_n2(far, 0)
    rs_e.send_far(0)
    ag_x.wait_third(1)
    unit(far, 1)
    unit_n2(far, 1)
    rs_e.send_far(1)
    unit_out(far, 0)
    unit_out(far, 1)

    outs = [(xall, x_out), (gal, g_out), (hid, hid_out), (dpre, dpre_out)]
    stores = [pltpu.make_async_copy(a, b, loc.at[6 + i]) for i, (a, b) in enumerate(outs)]
    for copy in stores:
        copy.start()

    rs_e.pass_on()
    rs_e.wait()
    rs_o.send_far(0)
    rs_o.send_far(1)
    rs_o.send_near(0)
    rs_o.send_near(1)

    def send_back(rs, buf, to):
        value = jnp.concatenate([rs.value(0), rs.value(1)], axis=0).astype(bf16)
        for c in range(4):
            chunk = rem4(me // 8 + c)
            row0 = pl.multiple_of(chunk * 128, 128)
            r = iota((128, 256), 0) + row0
            sel = hot(((r >> 2) & 1) * 128 + (r >> 4) * 4 + (r & 3) == iota((128, 256), 1))
            buf[pl.ds(row0, 128), :] = pick_halves(mm(sel, value), row0)
            start_chunk(to, chunk)

    def to_tokens(buf):
        slots = slot_c[...]
        target = (slots >> 3) * 16 + (slots & 7)
        lanes = iota((Q, T), 1)
        low = mm(hot(lanes == target), buf[...])
        return jnp.concatenate([low, mm(hot(lanes == target + 8), buf[...])], axis=1)

    e_to, e_arrived = row_copy(esend, erecv, es, er)
    o_to, o_arrived = row_copy(osend, orecv, os_, or_)
    send_back(rs_e, esend, e_to)
    erecv[own16, :] = esend[own16, :]

    sel_own = hot(iota((Q, T), 0) + h * Q == iota((Q, T), 1))
    cot_q = mm(mm(sel_own, pm[...]).astype(bf16), cot_low[...])
    others(lambda d: e_arrived(d).wait_recv())
    dn2 = to_tokens(erecv)
    xhat2, r2 = resid_norm()
    nv[2] = as_tile(jnp.sum(dn2 * xhat2, axis=0, keepdims=True))
    nv[3] = as_tile(jnp.sum(dn2, axis=0, keepdims=True))
    d_resid = cot_q + norm_back(dn2 * g2_ref[...], xhat2, r2)
    dres[...] = d_resid
    datt[own_rows, :] = d_resid.astype(bf16)
    ag_d = Gather(ring_x, columns(datt, Q), ags.at[1], agr.at[1])
    ag_d.start()
    ag_d.finish()

    dmx[...] = mm_nt(datt[...], wout[...]).astype(bf16)
    dm_t[...] = dmx[...].astype(f32).T.astype(bf16)

    @pl.loop(0, 4)
    def _(c):
        cols = pl.ds(pl.multiple_of(c * 256, 256), 256)
        rows = pl.ds(pl.multiple_of(c * 256, 256), 256)
        wpart[rows, 768:1024] = mm(mixed_t[...], datt[:, cols]).astype(bf16)

    rs_o.pass_on()

    for hp in range(2):
        pair = slice(hp * 128, hp * 128 + 128)

        @pl.loop(0, 4)
        def _(rb):
            rows = pl.ds(pl.multiple_of(rb * Q, Q), Q)
            dqs = []
            for hh in range(2):
                lanes = slice(hp * 128 + hh * 64, hp * 128 + hh * 64 + 64)
                dch = mm_nt(dmx[rows, lanes], qkv[2, :, lanes])
                ch = chs[hp * 2 + hh, rows, :].astype(f32)
                inner = jnp.sum(ch * dch, axis=-1, keepdims=True)
                ds = (ch * (dch - inner)).astype(bf16)
                dss[hh][rows, :] = ds
                dqs.append(mm(ds, qkv[1, :, lanes]) * 0.125)
            dqkv[0, rows, pair] = jnp.concatenate(dqs, axis=1).astype(bf16)

        dks, dvs = [], []
        for hh in range(2):
            lanes = slice(hp * 128 + hh * 64, hp * 128 + hh * 64 + 64)
            dks.append(mm(q_t[lanes, :], dss[hh][...]) * 0.125)
            dvs.append(mm(dm_t[lanes, :], chs[hp * 2 + hh]))
        dqkv[1, :, pair] = jnp.concatenate(dks, axis=0).T.astype(bf16)
        dqkv[2, :, pair] = jnp.concatenate(dvs, axis=0).T.astype(bf16)
        if hp == 0:
            rs_o.wait()
            send_back(rs_o, osend, o_to)
            orecv[own16, :] = osend[own16, :]

    rs_d = ReduceScatter(
        ring_x, columns(npart, Q), halves(d_rel), halves(d_sum), sides(d_arr), rss.at[3], rsr.at[3]
    )

    def input_grad(b):
        rows = pl.ds(pl.multiple_of(b * Q, Q), Q)
        total = mm_nt(dqkv[0, rows, :], wqkv[0])
        for c in (1, 2):
            total += mm_nt(dqkv[c, rows, :], wqkv[c])
        npart[rows, :] = total.astype(bf16)

    input_grad(far)
    rs_d.send_far(0)
    rs_d.send_far(1)
    input_grad(left)
    rs_d.send_near(0)
    input_grad(right)
    rs_d.send_near(1)
    input_grad(h)

    for c in range(3):
        wpart[:, c * 256 : (c + 1) * 256] = mm(normed_t[...], dqkv[c]).astype(bf16)

    core_rows = pl.ds(pl.multiple_of(core * T, T), T)
    other_rows = pl.ds(pl.multiple_of((1 - core) * T, T), T)
    swap = remote(wpart.at[other_rows, :], wx, xs.at[0], xr.at[0], sibling)
    swap.start()
    rs_d.pass_on()
    swap.wait_recv()
    ws[...] = (wpart[core_rows, :].astype(f32) + wx[...].astype(f32)).astype(bf16)
    ws0, ws1 = ws.at[pl.ds(0, 256), :], ws.at[pl.ds(256, 256), :]
    rs_w0 = ReduceScatter(
        ring_y, columns(ws0, 64), halves(w0_rel), halves(w0_sum), sides(w0_arr), rss.at[4], rsr.at[4]
    )
    rs_w1 = ReduceScatter(
        ring_z, columns(ws1, 64), halves(w1_rel), halves(w1_sum), sides(w1_arr), rss.at[5], rsr.at[5]
    )
    rs_w2 = ReduceScatter(
        ring_z, columns(w0, 16), halves(w2_rel), halves(w2_sum), sides(w2_arr), rss.at[6], rsr.at[6]
    )
    rs_w3 = ReduceScatter(
        ring_y, columns(w1, 16), halves(w3_rel), halves(w3_sum), sides(w3_arr), rss.at[7], rsr.at[7]
    )

    def start_all(rs):
        rs.send_far(0)
        rs.send_far(1)
        rs.send_near(0)
        rs.send_near(1)

    start_all(rs_w0)
    start_all(rs_w1)

    others(lambda d: o_arrived(d).wait_recv())
    outall[own_rows, :] = (att_q[...] + to_tokens(orecv)).astype(bf16)
    ag_o = Gather(ring_x, columns(outall, Q), ags.at[2], agr.at[2])

    rs_d.wait()
    dn1 = jnp.concatenate([rs_d.value(0), rs_d.value(1)], axis=1)
    xhat1, r1 = norm_parts(xp[own_rows, :].astype(f32))
    gtall[own_rows, :] = (dres[...] + norm_back(dn1 * g1_ref[...], xhat1, r1)).astype(bf16)
    ag_g = Gather(ring_x, columns(gtall, Q), ags.at[3], agr.at[3])
    ag_g.start()
    ag_o.start()
    nv[0] = as_tile(jnp.sum(dn1 * xhat1, axis=0, keepdims=True))
    nv[1] = as_tile(jnp.sum(dn1, axis=0, keepdims=True))

    nx = [remote(nv.at[rem4(h + k)], nrx.at[h], vs.at[k], vr.at[h], {"head": rem4(h + k)})
          for k in (1, 2, 3)]
    nx_in = [remote(nv.at[0], nrx.at[rem4(h + k)], vs.at[k], vr.at[rem4(h + k)], {"head": rem4(h + k)})
             for k in (1, 2, 3)]
    for copy in nx:
        copy.start()

    rs_w0.pass_on()
    rs_w1.pass_on()
    ag_g.pass_on(0)
    ag_g.pass_on(1)

    for copy in nx_in:
        copy.wait_recv()
    nye[me] = nv[h] + nrx[rem4(h + 1)] + nrx[rem4(h + 2)] + nrx[rem4(h + 3)]

    def n_all(d):
        return remote(nye.at[me], nye.at[me], vys.at[d], vyr.at[me], {"expert": d})

    def n_all_in(d):
        return remote(nye.at[me], nye.at[d], vys.at[d], vyr.at[d], {"expert": d})

    others(lambda d: n_all(d).start())

    rs_w0.wait()
    w0[...] = jnp.concatenate([rs_w0.value(0), rs_w0.value(1)], axis=1).astype(bf16)
    start_all(rs_w2)
    rs_w1.wait()
    w1[...] = jnp.concatenate([rs_w1.value(0), rs_w1.value(1)], axis=1).astype(bf16)
    start_all(rs_w3)
    ag_o.pass_on(0)
    ag_o.pass_on(1)
    rs_w2.pass_on()
    rs_w3.pass_on()

    base = core * T
    row_y = pl.multiple_of(base + y * 64, 64)
    row_z = pl.multiple_of(base + 256 + z * 64, 64)
    ag_w2 = Gather(ring_z, columns(w_out.at[pl.ds(row_y, 64), :], 16), ags.at[4], agr.at[4])
    ag_w3 = Gather(ring_y, columns(w_out.at[pl.ds(row_z, 64), :], 16), ags.at[5], agr.at[5])
    ag_w0 = Gather(
        ring_y, columns(w_out.at[pl.ds(pl.multiple_of(base, 256), 256), :], 64), ags.at[6], agr.at[6]
    )
    ag_w1 = Gather(
        ring_z, columns(w_out.at[pl.ds(pl.multiple_of(base + 256, 256), 256), :], 64), ags.at[7], agr.at[7]
    )
    rs_w2.wait()
    w_out[pl.ds(pl.multiple_of(row_y + z * 16, 16), 16), :] = jnp.concatenate(
        [rs_w2.value(0), rs_w2.value(1)], axis=1
    ).astype(bf16)
    ag_w2.start()
    rs_w3.wait()
    w_out[pl.ds(pl.multiple_of(row_z + y * 16, 16), 16), :] = jnp.concatenate(
        [rs_w3.value(0), rs_w3.value(1)], axis=1
    ).astype(bf16)
    ag_w3.start()

    others(lambda d: n_all_in(d).wait_recv())
    nrm_out[h] = jnp.sum(nye[...], axis=0)
    nf = [remote(nrm_out.at[h], nrm_out.at[h], vs.at[3 + k], vr.at[4 + h], {"head": rem4(h + k)})
          for k in (1, 2, 3)]
    nf_in = [
        remote(nrm_out.at[h], nrm_out.at[rem4(h + k)], vs.at[3 + k], vr.at[4 + rem4(h + k)],
               {"head": rem4(h + k)})
        for k in (1, 2, 3)
    ]
    for copy in nf:
        copy.start()

    ag_w2.finish()
    ag_w0.start()
    ag_w3.finish()
    ag_w1.start()

    for hf in range(2):
        ag_g.wait_second(hf)
        ag_g.wait_third(hf)

    def restore(dst, src):
        @pl.loop(0, 4)
        def _(c):
            cols = pl.ds(pl.multiple_of(c * 256, 256), 256)
            dst[:, cols] = mm(pmt[...], src[:, cols]).astype(bf16)

    restore(xp, gtall)
    gt_store = pltpu.make_async_copy(xp, gt_out, loc.at[10])
    gt_store.start()
    ag_w0.finish()
    ag_w1.finish()
    both = remote(w_out.at[core_rows, :], w_out.at[core_rows, :], xs.at[1], xr.at[1], sibling)
    both_in = remote(w_out.at[core_rows, :], w_out.at[other_rows, :], xs.at[1], xr.at[1], sibling)
    both.start()
    for hf in range(2):
        ag_o.wait_second(hf)
        ag_o.wait_third(hf)
    restore(normed, outall)
    u_store = pltpu.make_async_copy(normed, u_out, loc.at[11])
    u_store.start()
    both_in.wait_recv()
    for copy in nf_in:
        copy.wait_recv()

    others(lambda d: n_to(d).wait_send())
    others(lambda d: e_to(d).wait_send())
    others(lambda d: o_to(d).wait_send())
    others(lambda d: n_all(d).wait_send())
    for group in (rs_a, rs_e, rs_o, rs_d, rs_w0, rs_w1, rs_w2, rs_w3,
                  ag_x, ag_d, ag_o, ag_g, ag_w0, ag_w1, ag_w2, ag_w3):
        group.wait_sent()
    swap.wait_send()
    both.wait_send()
    for copy in nx + nf:
        copy.wait_send()
    for copy in stores + [gt_store, u_store]:
        copy.wait()


def layer(seg, route, g1, b1, g2, b2, tok, wqkv, wout, win, wbk, cot):
    vmem = pl.BlockSpec(memory_space=pltpu.VMEM)
    hbm = pl.BlockSpec(memory_space=pl.ANY)
    V = pltpu.VMEM
    DMA = pltpu.SemaphoreType.DMA

    def rs_bufs(rows, cols):
        return [V((2, rows, cols), bf16), V((2, rows, cols), bf16), V((2, 2, rows, cols), bf16)]

    scratch = [
        V((T, D), bf16), V((3, D, 256), bf16), V((256, D), bf16), V((2, D, D), bf16),
        V((2, D, D), bf16), V((T, D), f32), V((T, D), bf16),
        V((T, T), bf16), V((T, T), bf16), V((T, 1), i32), V((1, T), i32), V((Q, 1), i32),
        V((1, Q), i32),
        V((2, T, D), bf16), V((2, T, D), bf16), V((4, 2, Q, D), bf16),
        V((T, D), bf16), V((T, D), bf16), V((D, T), bf16), V((3, T, 256), bf16),
        V((256, T), bf16), V((4, T, T), bf16), V((T, 256), bf16), V((256, T), bf16),
        V((T, D), bf16), *rs_bufs(Q, HALF),
        V((T, HALF), bf16), V((T, HALF), bf16), *[V((4, 2, Q, D), bf16)] * 4,
        *rs_bufs(Q, D), V((T, HALF), bf16), V((T, HALF), bf16),
        *rs_bufs(Q, D), V((T, HALF), bf16), V((T, HALF), bf16), V((T, D), bf16),
        V((T, D), bf16), V((T, 256), bf16), V((256, T), bf16), V((3, T, 256), bf16),
        *rs_bufs(Q, HALF), V((T, D), bf16),
        V((D, D), bf16), V((T, D), bf16), V((T, D), bf16),
        V((64, D), bf16), *rs_bufs(64, HALF), V((64, D), bf16), *rs_bufs(64, HALF),
        *rs_bufs(16, HALF), *rs_bufs(16, HALF),
        V((4, 8, 128), f32), V((4, 8, 128), f32), V((G, 8, 128), f32),
        DMA((12,)), *[DMA((G,))] * 8, *[DMA((8, 6))] * 4, DMA((2,)), DMA((2,)),
        DMA((8,)), DMA((8,)), DMA((G,)), DMA((G,)),
    ]
    S = jax.ShapeDtypeStruct
    quarters = S((4, 2, Q, D), bf16)
    return pl.pallas_call(
        layer_kernel,
        name="layer",
        out_shape=[quarters] * 4
        + [S((T, D), bf16), S((T, D), bf16), S((D, D), bf16), S((4, 8, 128), f32)],
        in_specs=[vmem] * 6 + [hbm] * 6,
        out_specs=[hbm] * 6 + [vmem] * 2,
        scratch_shapes=scratch,
        compiler_params=pltpu.CompilerParams(
            collective_id=0, has_side_effects=True, vmem_limit_bytes=62 << 20
        ),
        cost_estimate=pl.CostEstimate(
            flops=24 * 10**9, bytes_accessed=30 * 2**20, transcendentals=4 * 10**6
        ),
    )(seg, route, g1, b1, g2, b2, tok, wqkv, wout, win, wbk, cot)


def outer_kernel(x_ref, dpre_ref, hid_ref, g_ref, win_out, wback_out):
    def outer(lhs, rhs, out):
        a = lhs[...].reshape(T, 256)
        b = rhs[...].reshape(T, D)
        out[0] = lax.dot_general(a, b, (((0,), (0,)), ((), ())), preferred_element_type=f32)

    outer(x_ref, dpre_ref, win_out)
    outer(hid_ref, g_ref, wback_out)


def expert_weight_grads(x, dpre, hid, g):
    lhs = pl.BlockSpec((4, 1, Q, 256), lambda e, c: (0, e, 0, c))
    rhs = pl.BlockSpec((4, 1, Q, D), lambda e, c: (0, e, 0, 0))
    out = pl.BlockSpec((1, 256, D), lambda e, c: (e, c, 0))
    shape = jax.ShapeDtypeStruct((2, D, D), f32)
    return pl.pallas_call(
        outer_kernel,
        name="expert_weight_grads",
        grid=(2, 4),
        out_shape=[shape, shape],
        in_specs=[lhs, rhs, lhs, rhs],
        out_specs=[out, out],
        compiler_params=pltpu.CompilerParams(vmem_limit_bytes=40 << 20),
        cost_estimate=pl.CostEstimate(
            flops=8 * 2**30, bytes_accessed=24 * 2**20, transcendentals=0
        ),
    )(x, dpre, hid, g)


def per_device(
    tokens, segment_ids, expert_of, norm1_gain, norm1_bias, norm2_gain, norm2_bias,
    w_qkv, w_out, w_in, w_back, cotangent,
):
    row = lambda v: v.reshape(1, D)
    x, g, hid, dpre, u, gt, w, nrm = layer(
        segment_ids, expert_of, row(norm1_gain), row(norm1_bias), row(norm2_gain), row(norm2_bias),
        tokens, w_qkv, w_out, w_in, w_back, cotangent,
    )
    grad_w_in, grad_w_back = expert_weight_grads(x, dpre, hid, g)
    output = tokens.astype(f32) + u.astype(f32)
    grad_tokens = gt.astype(f32)
    w = w.astype(f32)
    grad_w_qkv = jnp.moveaxis(w[:, :768].reshape(D, 3, 256), 1, 0)
    grad_w_out = jnp.moveaxis(w[:, 768:].reshape(4, 256, 256), 0, 1).reshape(256, D)
    vectors = nrm.reshape(4, D)
    return (
        output, grad_tokens, vectors[0], vectors[1], vectors[2], vectors[3],
        grad_w_qkv, grad_w_out, grad_w_in, grad_w_back,
    )


def solution(mesh):
    return jax.shard_map(
        per_device,
        mesh=mesh,
        in_specs=(
            P("expert", None),
            P("expert", None),
            P("expert", None),
            P(),
            P(),
            P(),
            P(),
            P(None, None, "head"),
            P("head", None),
            P("expert", None, "head"),
            P("expert", "head", None),
            P("expert", None),
        ),
        out_specs=(
            P("expert", None),
            P("expert", None),
            P(),
            P(),
            P(),
            P(),
            P(None, None, "head"),
            P("head", None),
            P("expert", None, "head"),
            P("expert", "head", None),
        ),
        check_vma=False,
    )
```

time: 498 us -> 224 us (0.45); the launches traced: 488 us -> 224 us
  waiting for transfers between devices: 220 us -> 0 us
  Pallas kernels: 0 us -> 202 us
  matrix products: 69.9 us -> 0 us
  blocking collectives: 65.5 us -> 0 us
  starting transfers between devices: 51.1 us -> 0 us
  other arithmetic: 40.9 us -> 3.27 us
  between operations: 14.8 us -> 0.69 us
  local copies, waits for them, and re-layouts: 26.3 us -> 17.5 us
    pallas_call x0 -> x2, Pallas kernels: none -> 202 us  [the longest x1 193 us: layer(): pl.pallas_call(layer_kernel, name='layer', out_shape=[quarters] * 4 + [S(...]
    psum x3 -> x0, waiting for transfers between devices: 111 us -> none  [the longest x1 41.6 us: per_device(): lax.psum(grad_w_qkv.astype(jnp.bfloat16), 'expert').astype(jnp.float32)]
    all_to_all x8 -> x0, waiting for transfers between devices: 109 us -> none  [the longest x2 34.8 us: sum_at_owner(): lax.all_to_all(blocks, axis, split_axis=0, concat_axis=0, tiled=True)]
    dot_general x22 -> x0, matrix products: 69.9 us -> none  [the longest x1 8.98 us: per_device(): jnp.einsum('nemf,nemd->efd', hidden_again, grad_recv, preferred_element_t...]
    psum x1 -> x0, blocking collectives: 65.5 us -> none  [per_device(): lax.psum(grad_gain1.astype(jnp.bfloat16), 'expert').astype(jnp.float32)]
    all_to_all x8 -> x0, starting transfers between devices: 50.8 us -> none  [the longest x1 12.4 us: per_device(): lax.all_to_all(share_grad, 'expert', split_axis=0, concat_axis=0, tiled=T...]
    reduce_sum x14 -> x0, other arithmetic: 21.9 us -> none  [the longest x5 6.79 us: layer_norm(): return center * lax.rsqrt(spread + 1e-05) * gain + bias]
    convert_element_type x8 -> x1, other arithmetic: 7.39 us -> 1.56 us  [per_device(): grad_tokens = gt.astype(f32)]
  transfers between devices with their start and end apart: 11 -> 0, of which waited for: 11 -> 0; matrix products, arithmetic and copies ran while one was open for 15% -> 0% of each run, Pallas kernels for 0% -> 0%
where the time goes in v1:
time: 224 us
  Pallas kernels  202 us (90%)
  local copies, waits for them, and re-layouts  17.5 us (8%)
  other arithmetic  3.27 us (1%)
    pallas_call x1, Pallas kernels, layer(): pl.pallas_call(layer_kernel, name='layer', out_shape=[quarters] * 4 + [S(...  193 us
    unnamed x20, local copies, waits for them, and re-layouts  10.3 us
    pallas_call x1, Pallas kernels, expert_weight_grads(): pl.pallas_call(outer_kernel, name='expert_weight_grads', grid=(2, 4), out...  8.65 us

profile of v1, /device:TPU:1, one launch (start us, length us, event | category | flops | bytes accessed | tf_op | source)
XLA Modules:
  0.0 223.6 jit_solution(4445043543037674693)
XLA Ops:
  0.6 1.5 copy.25.route_ref
  2.2 193.4 %layer.1 = (bf16[4,2,128,1024]{3,2,1,0:T(8,128)(2,1)}, bf16[4,2,128,1024]{3,2,1,0:T(8,128)(2,1)}, bf16[4,2,128,1024]{3,2,1,0:T(8,128)(2,1)}, bf16[4,2,128,1024]{...) custom-call(s32[1,512]{1,0:T(1,128)} %seg_ref.1, ...), custom_call_target="tpu_custom_call" | custom-call | flops 24000000000 | bytes 31457280 | tf_op jit(solution)/shard_map/layer/pallas_call | solution.py:803
  195.6 0.0 copy-start
  195.6 1.6 copy-done
  197.2 0.0 copy-start.1
  197.2 1.6 copy-done.1
  198.8 0.0 copy-start.2
  198.8 1.6 copy-done.2
  200.4 0.0 copy-start.3
  200.4 1.6 copy-done.3
  202.0 0.0 copy-start.8
  202.0 0.0 copy-start.4
  202.0 8.7 %expert_weight_grads.1 = (f32[2,1024,1024]{2,1,0:T(8,128)}, f32[2,1024,1024]{2,1,0:T(8,128)}) custom-call(bf16[4,2,128,1024]{3,2,1,0:T(8,128)(2,1)S(1)} %copy-done, bf16[4,2,128,1024]{3,2,1,0:T(8,128)(2,1)S(1)} %copy-done.3, bf16[4,2,128,1024]{3,2,1,0:T(8,128)(2,1)S(1)} %copy-done.2, bf16[4,2,128,1024]{3,2,1,0:T(8,128)(2,1)S(1)} %copy-done.1), custom_call_target="tpu_custom_call" | custom-call | flops 8589934592 | bytes 25165824 | tf_op jit(solution)/shard_map/expert_weight_grads/pallas_call | solution.py:835
  210.6 0.0 copy-done.8
  210.6 0.6 slice_bitcast_fusion
  211.2 0.0 copy-done.4
  211.2 1.9 slice.28
  213.1 2.4 %copy.26 = f32[1024,768]{0,1:T(8,128)S(1)} copy(f32[1024,768]{1,0:T(8,128)} %slice.28) | data formatting | bytes 6291456 | tf_op jit(solution)/shard_map/slice | solution.py:862
  215.5 2.4 %copy.28 = f32[3,1024,256]{2,1,0:T(8,128)} copy(f32[3,1024,256]{1,2,0:T(8,128)S(1)} %bitcast.20) | data formatting | bytes 6291456
  217.9 0.0 copy-start.6
  217.9 0.0 copy-start.7
  217.9 1.3 slice.29
  219.2 1.1 copy.29
  220.3 0.0 copy-done.6
  220.3 0.0 copy-done.7
  220.3 0.0 copy-start.5
  220.3 1.7 convert_add_fusion
  222.0 0.0 copy-done.5
  222.0 1.6 convert_element_type.14
Async XLA Ops:
  195.6 1.6 copy-start
  197.2 1.6 copy-start.1
  198.8 1.6 copy-start.2
  200.4 1.6 copy-start.3
  202.0 8.7 %copy-start.8 = (f32[4,8,128]{2,1,0:T(8,128)S(1)}, f32[4,8,128]{2,1,0:T(8,128)}, u32[]{:S(2)}) copy-start(f32[4,8,128]{2,1,0:T(8,128)} %get-tuple-element.22) | copy-start | bytes 49156
  202.0 9.3 %copy-start.4 = (bf16[1024,1024]{1,0:T(8,128)(2,1)S(1)}, bf16[1024,1024]{1,0:T(8,128)(2,1)}, u32[]{:S(2)}) copy-start(bf16[1024,1024]{1,0:T(8,128)(2,1)} %get-tuple-element.23) | copy-start | bytes 6291460
  217.9 2.4 %copy-start.6 = (bf16[512,1024]{1,0:T(8,128)(2,1)S(1)}, bf16[512,1024]{1,0:T(8,128)(2,1)}, u32[]{:S(2)}) copy-start(bf16[512,1024]{1,0:T(8,128)(2,1)} %tok_hbm.1) | copy-start | bytes 3145732
  217.9 2.4 %copy-start.7 = (bf16[512,1024]{1,0:T(8,128)(2,1)S(1)}, bf16[512,1024]{1,0:T(8,128)(2,1)}, u32[]{:S(2)}) copy-start(bf16[512,1024]{1,0:T(8,128)(2,1)} %get-tuple-element.20) | copy-start | bytes 3145732
  220.3 1.7 copy-start.5

commit v2 on v1

v2 whole, which is shorter than its diff:
```python
import functools

import jax
import jax.numpy as jnp
from jax import lax
from jax.experimental import pallas as pl
from jax.experimental.pallas import tpu as pltpu
from jax.sharding import PartitionSpec as P

f32 = jnp.float32
bf16 = jnp.bfloat16
i32 = jnp.int32
MESH = pl.DeviceIdType.MESH

T = 512
D = 1024
G = 32
H = 4
Q = T // H
HALF = D // 2
EPS = 1e-5


def mm(a, b):
    return lax.dot_general(a, b, (((1,), (0,)), ((), ())), preferred_element_type=f32)


def mm_nt(a, b):
    return lax.dot_general(a, b, (((1,), (1,)), ((), ())), preferred_element_type=f32)


def iota(shape, dim):
    return lax.broadcasted_iota(i32, shape, dim)


def hot(cond):
    return jnp.where(cond, 1.0, 0.0).astype(bf16)


def rem4(v):
    return lax.rem(v, 4)


def remote(src, dst, send_sem, recv_sem, device):
    return pltpu.make_async_remote_copy(
        src_ref=src,
        dst_ref=dst,
        send_sem=send_sem,
        recv_sem=recv_sem,
        device_id=device,
        device_id_type=MESH,
    )


def columns(ref, rows):
    half = ref.shape[1] // 2
    return lambda b, hf: ref.at[pl.ds(pl.multiple_of(b * rows, rows), rows), pl.ds(hf * half, half)]


class ReduceScatter:
    def __init__(self, ring, whole, rows, relay, total, arrived, sems):
        self.me, right, left = ring
        self.right, self.left = rem4(self.me + 1), rem4(self.me + 3)
        far = rem4(self.me + 2)
        self.part = part = columns(whole, rows)
        self.relay, self.total, self.arrived = relay, total, arrived
        self.three, self.two = whole.at[pl.ds(0, 3 * rows), :], whole.at[pl.ds(0, 2 * rows), :]
        self.sems, self.left_device = sems, left
        send, rest = sems.at[0], sems.at[3]
        self.far = [
            remote(part(far, 0), relay.at[0], send, sems.at[1], left),
            remote(part(far, 1), relay.at[1], send, sems.at[2], right),
        ]
        self.near = [
            remote(part(self.left, 1), arrived.at[1, 1], send, rest, left),
            remote(part(self.right, 0), arrived.at[0, 0], send, rest, right),
        ]
        self.last = [
            remote(total.at[0], arrived.at[1, 0], send, rest, left),
            remote(total.at[1], arrived.at[0, 1], send, rest, right),
        ]

    def send_all(self):
        for copy in self.far + self.near:
            copy.start()

    def pass_on(self):
        for hf, owner in ((0, self.left), (1, self.right)):
            self.far[hf].wait_recv()
            mine = self.part(owner, hf)[...].astype(f32)
            self.total[hf] = (mine + self.relay[hf].astype(f32)).astype(bf16)
            self.last[hf].start()

    def wait(self):
        all_of(self.two, self.sems.at[0], self.sems.at[3], self.left_device).wait_recv()

    def value(self):
        def half(hf):
            mine = self.part(self.me, hf)[...].astype(f32)
            return mine + self.arrived[0, hf].astype(f32) + self.arrived[1, hf].astype(f32)

        return jnp.concatenate([half(0), half(1)], axis=1)

    def wait_sent(self):
        all_of(self.three, self.sems.at[0], self.sems.at[3], self.left_device).wait_send()


class Gather:
    def __init__(self, ring, whole, rows, sems):
        me, right, left = ring
        on_right, on_left = rem4(me + 1), rem4(me + 3)
        block = columns(whole, rows)
        self.three, self.two = whole.at[pl.ds(0, 3 * rows), :], whole.at[pl.ds(0, 2 * rows), :]
        self.sems, self.left_device = sems, left

        def copy(b, hf, i, device):
            return remote(block(b, hf), block(b, hf), sems.at[0], sems.at[i], device)

        self.first = [copy(me, 0, 1, right), copy(me, 1, 2, left)]
        self.second = [copy(me, 0, 3, left), copy(me, 1, 3, right)]
        self.third = [copy(on_left, 0, 3, right), copy(on_right, 1, 3, left)]

    def start(self):
        for copy in self.first + self.second:
            copy.start()

    def pass_on(self):
        for hf in range(2):
            self.first[hf].wait_recv()
            self.third[hf].start()

    def wait_rest(self):
        all_of(self.two, self.sems.at[0], self.sems.at[3], self.left_device).wait_recv()

    def finish(self):
        self.pass_on()
        self.wait_rest()

    def wait_sent(self):
        all_of(self.three, self.sems.at[0], self.sems.at[3], self.left_device).wait_send()


class Exchange:
    def __init__(self, me, src, dst, sems):
        self.me, self.src, self.dst, self.sems = me, src, dst, sems
        rows = pl.ds(0, 16 * (G - 1))
        index = (slice(None),) * (len(src.shape) - 2) + (rows, slice(None))
        other = {"expert": lax.rem(me + 1, G)}
        self.all = remote(src.at[index], dst.at[index], sems.at[0], sems.at[1], other)

    def block(self, ref, d):
        rows = pl.ds(pl.multiple_of(d * 16, 16), 16)
        return ref.at[(slice(None),) * (len(ref.shape) - 2) + (rows, slice(None))]

    def start_chunk(self, chunk):
        @pl.loop(0, 8)
        def _(k):
            d = chunk * 8 + lax.rem(self.me + k, 8)

            @pl.when(d != self.me)
            def _():
                remote(
                    self.block(self.src, d), self.block(self.dst, self.me),
                    self.sems.at[0], self.sems.at[1], {"expert": d},
                ).start()

    def keep_own(self):
        self.block(self.dst, self.me)[...] = self.block(self.src, self.me)[...]


def all_of(view, send_sem, recv_sem, device):
    return remote(view, view, send_sem, recv_sem, device)


def norm_parts(x):
    center = x - jnp.mean(x, axis=-1, keepdims=True)
    r = lax.rsqrt(jnp.mean(center * center, axis=-1, keepdims=True) + EPS)
    return center * r, r


def norm_back(g, xhat, r):
    return r * (
        g - jnp.mean(g, axis=-1, keepdims=True) - xhat * jnp.mean(g * xhat, axis=-1, keepdims=True)
    )


def gelu_parts(v):
    c = 0.7978845608028654
    v2 = v * v
    t = jnp.tanh(c * v * (1.0 + 0.044715 * v2))
    half = 0.5 * (1.0 + t)
    grad = half + 0.5 * v * (1.0 - t * t) * c * (1.0 + 3.0 * 0.044715 * v2)
    return v * half, grad


def as_tile(row):
    return jnp.concatenate([row[:, i * 128 : (i + 1) * 128] for i in range(8)], axis=0)


def layer_kernel(
    seg_ref, route_ref, g1_ref, b1_ref, g2_ref, b2_ref,
    tok_hbm, wqkv_hbm, wout_hbm, win_hbm, wbk_hbm, cot_hbm,
    x_out, g_out, hid_out, dpre_out, u_out, gt_out, w_out, nrm_out,
    tok, wqkv, wout, win, wbk, cotw, cot_low,
    pm, pmt, code_c, code_r, slot_c, slot_r,
    csend, crecv, gal,
    xp, normed, normed_t, qkv, q_t, chs, mixed, mixed_t,
    apart, a_rel, a_sum, a_arr,
    norm2, nsend, nrecv, xall, hid, dpre, n2p,
    e_rel, e_sum, e_arr, esend, erecv,
    o_rel, o_sum, o_arr, osend, orecv, outall,
    datt, dmx, dm_t, dqkv,
    d_rel, d_sum, d_arr, gtall,
    wx,
    w0, w0_rel, w0_sum, w0_arr, w1, w1_rel, w1_sum, w1_arr,
    w2_rel, w2_sum, w2_arr, w3_rel, w3_sum, w3_arr,
    nv, nrx, nye,
    loc, cs, ns, es, os_, rss, ags, xs, vs,
):
    me = lax.axis_index("expert")
    h = lax.axis_index("head")
    core = lax.rem(me, 2)
    chip = me // 2
    y = lax.rem(chip, 4)
    z = chip // 4

    def at_yz(yy, zz, cc):
        return {"expert": (rem4(zz) * 4 + rem4(yy)) * 2 + cc}

    ring_x = (h, {"head": rem4(h + 1)}, {"head": rem4(h + 3)})
    ring_y = (y, at_yz(y + 1, z, core), at_yz(y + 3, z, core))
    ring_z = (z, at_yz(y, z + 1, core), at_yz(y, z + 3, core))
    sibling = {"expert": chip * 2 + 1 - core}
    left, right, far = rem4(h + 3), rem4(h + 1), rem4(h + 2)

    att_q, dres = cotw.at[pl.ds(0, Q), :], cotw.at[pl.ds(Q, Q), :]
    npart = tok
    ws = cot_low
    wpart = gal
    dss = [tok.at[:, pl.ds(0, T)], tok.at[:, pl.ds(T, T)]]
    outp = csend

    loads = {}
    for i, (name, src, dst) in enumerate(
        (
            ("cot", cot_hbm, cotw),
            ("tok", tok_hbm, tok),
            ("wqkv", wqkv_hbm, wqkv),
            ("wout", wout_hbm, wout),
            ("win", win_hbm, win),
            ("wbk", wbk_hbm, wbk),
        )
    ):
        loads[name] = pltpu.make_async_copy(src, dst, loc.at[i])
        loads[name].start()

    barrier = pltpu.get_barrier_semaphore()

    @pl.loop(1, G)
    def _(k):
        pl.semaphore_signal(
            barrier, inc=1, device_id={"expert": lax.rem(me + k, G)}, device_id_type=MESH
        )

    for k in range(1, H):
        pl.semaphore_signal(barrier, inc=1, device_id={"head": rem4(h + k)}, device_id_type=MESH)

    eye = iota((T, T), 0) == iota((T, T), 1)
    route_row = route_ref[...].astype(f32)
    route_c = jnp.sum(jnp.where(eye, route_row, 0.0), axis=1, keepdims=True).astype(i32)

    def to_row(col):
        return jnp.sum(jnp.where(eye, col.astype(f32), 0.0), axis=0, keepdims=True)

    onehot = jnp.where(iota((T, 128), 1) == route_c, 1.0, 0.0)
    before = hot(iota((T, T), 1) < iota((T, T), 0))
    rank = jnp.sum(mm(before, onehot.astype(bf16)) * onehot, axis=1, keepdims=True)
    count = jnp.broadcast_to(jnp.sum(onehot, axis=0, keepdims=True), (8, 128)).astype(bf16)
    first = mm(count, hot(iota((128, 128), 0) < iota((128, 128), 1)))[0:1]
    place = (jnp.sum(onehot * first, axis=1, keepdims=True) + rank).astype(i32)
    rank4 = rank.astype(i32) >> 2
    quarter = place & 3
    pos_c = quarter * Q + (place >> 2)
    slot4 = route_c * 4 + rank4
    key = (route_c & 1) * T + (route_c >> 1) * 16 + quarter * 4 + rank4
    pos_r = to_row(pos_c).astype(i32)
    key_r = to_row(key).astype(i32)
    perm = iota((T, T), 0) == pos_r
    perm_t = iota((T, T), 1) == pos_c
    pm[...] = hot(perm)
    pmt[...] = hot(perm_t)
    code = (seg_ref[...] * 1024 + iota((1, T), 1)).astype(f32)
    code_pc = jnp.sum(jnp.where(perm, code, 0.0), axis=1, keepdims=True)
    code_c[...] = code_pc.astype(i32)
    code_r[...] = to_row(code_pc).astype(i32)
    own_t = iota((T, Q), 1) + h * Q == pos_c
    slot_row = jnp.sum(jnp.where(own_t, slot4.astype(f32), 0.0), axis=0, keepdims=True)
    slot_r[...] = slot_row.astype(i32)
    eye_q = iota((Q, Q), 0) == iota((Q, Q), 1)
    slot_c[...] = jnp.sum(jnp.where(eye_q, slot_row, 0.0), axis=1, keepdims=True).astype(i32)

    pl.semaphore_wait(barrier, G - 1 + H - 1)

    loads["cot"].wait()
    cot_low[...] = cotw[...].astype(bf16)

    def others(act):
        @pl.loop(1, G)
        def _(k):
            act(lax.rem(me + k, G))

    def exchange(src, dst, sems):
        return [Exchange(me, src.at[e], dst.at[e], sems.at[e]) for e in range(2)]

    cot_x = Exchange(me, csend, crecv, cs)

    @pl.loop(0, 4)
    def _(c):
        chunk = rem4(me // 8 + c)
        row0 = pl.multiple_of(chunk * 128, 128)
        r = iota((256, T), 0)
        sel = hot(row0 + (r & 127) + (r >> 7) * T == key_r)
        rows = mm(sel, cot_low[...]).astype(bf16)
        for e in range(2):
            csend[e, pl.ds(row0, 128), :] = rows[e * 128 : e * 128 + 128]
        cot_x.start_chunk(chunk)

    cot_x.keep_own()

    loads["tok"].wait()

    @pl.loop(0, 4)
    def _(rb):
        rows = pl.ds(pl.multiple_of(rb * Q, Q), Q)
        x = mm(pm[rows, :], tok[...])
        xp[rows, :] = x.astype(bf16)
        xhat, _r = norm_parts(x)
        normed[rows, :] = (xhat * g1_ref[...] + b1_ref[...]).astype(bf16)

    loads["wqkv"].wait()

    @pl.loop(0, 3)
    def _(c):
        qkv[c] = mm(normed[...], wqkv[c]).astype(bf16)

    for hp in range(2):
        pair = slice(hp * 128, hp * 128 + 128)

        @pl.loop(0, 4)
        def _(rb):
            rows = pl.ds(pl.multiple_of(rb * Q, Q), Q)
            codes = code_c[rows, :]
            keys = code_r[...]
            allowed = (keys <= codes) & (keys >= ((codes >> 10) << 10))
            outs = []
            for hh in range(2):
                lanes = slice(hp * 128 + hh * 64, hp * 128 + hh * 64 + 64)
                s = mm_nt(qkv[0, rows, lanes], qkv[1, :, lanes]) * 0.125
                s = jnp.where(allowed, s, -1e30)
                e = jnp.exp(s - jnp.max(s, axis=-1, keepdims=True))
                ch = (e * (1.0 / jnp.sum(e, axis=-1, keepdims=True))).astype(bf16)
                chs[hp * 2 + hh, rows, :] = ch
                outs.append(mm(ch, qkv[2, :, lanes]))
            mixed[rows, pair] = jnp.concatenate(outs, axis=1).astype(bf16)

    loads["wout"].wait()
    rs_a = ReduceScatter(ring_x, apart, Q, a_rel, a_sum, a_arr, rss.at[0])

    def project(b):
        rows = pl.ds(pl.multiple_of(b * Q, Q), Q)
        apart[rows, :] = mm(mixed[rows, :], wout[...]).astype(bf16)

    project(far)
    for copy in rs_a.far:
        copy.start()
    project(left)
    rs_a.near[0].start()
    project(right)
    rs_a.near[1].start()
    project(h)
    own_rows = pl.ds(pl.multiple_of(h * Q, Q), Q)

    rs_a.pass_on()
    q_t[...] = qkv[0].astype(f32).T.astype(bf16)
    mixed_t[...] = mixed[...].astype(f32).T.astype(bf16)

    @pl.loop(0, 4)
    def _(c):
        cols = pl.ds(pl.multiple_of(c * 256, 256), 256)
        normed_t[cols, :] = normed[:, cols].astype(f32).T.astype(bf16)

    rs_a.wait()
    att_q[...] = rs_a.value()

    def resid_norm():
        return norm_parts(xp[own_rows, :].astype(f32) + att_q[...])

    xhat2, _r2 = resid_norm()
    norm2[...] = (xhat2 * g2_ref[...] + b2_ref[...]).astype(bf16)
    n_x = exchange(nsend, nrecv, ns)

    def pick_quarter(full):
        cq = (iota((128, 256), 0) >> 2) & 3
        out = full[:, :256]
        for k in (1, 2, 3):
            out = jnp.where(cq == k, full[:, k * 256 : (k + 1) * 256], out)
        return out.astype(bf16)

    for e in range(2):

        @pl.loop(0, 4)
        def _(c):
            chunk = rem4(me // 8 + c)
            row0 = pl.multiple_of(chunk * 128, 128)
            r = iota((128, Q), 0) + row0
            sel = hot((r >> 4) * 8 + e * 4 + (r & 3) == slot_r[...])
            nsend[e, pl.ds(row0, 128), :] = pick_quarter(mm(sel, norm2[...]))
            n_x[e].start_chunk(chunk)

        n_x[e].keep_own()

    cot_x.all.wait_recv()

    i = iota((T, T), 0)
    reorder = hot(((i & 127) >> 2) * 16 + (i >> 7) * 4 + (i & 3) == iota((T, T), 1))
    for e in range(2):

        @pl.loop(0, 4)
        def _(c):
            cols = pl.ds(pl.multiple_of(c * 256, 256), 256)
            gal[e, :, cols] = mm(reorder, crecv[e, :, cols]).astype(bf16)

    ag_x = [Gather(ring_x, xall.at[e], Q, ags.at[e]) for e in range(2)]

    def compact(e):
        n_x[e].all.wait_recv()
        i = iota((Q, T), 0)
        target = (i >> 2) * 16 + (i & 3)
        for cq in range(4):
            sel = hot(iota((Q, T), 1) == target + cq * 4)
            xall[e, own_rows, cq * 256 : (cq + 1) * 256] = mm(sel, nrecv[e]).astype(bf16)

    compact(0)
    ag_x[0].start()
    compact(1)
    ag_x[0].pass_on()
    ag_x[1].start()

    loads["win"].wait()
    loads["wbk"].wait()
    cot_x.all.wait_send()

    def unit(e):
        @pl.loop(0, 2)
        def _(c):
            cols = pl.ds(pl.multiple_of(c * 512, 512), 512)
            act, slope = gelu_parts(mm(xall[e], win[e, :, cols]))
            hid[e, :, cols] = act.astype(bf16)
            dpre[e, :, cols] = (mm_nt(gal[e], wbk[e, cols, :]) * slope).astype(bf16)

    def unit_n2(e):
        @pl.loop(0, 2)
        def _(c):
            cols = pl.ds(pl.multiple_of(c * 512, 512), 512)
            n2p[e, :, cols] = mm_nt(dpre[e], win[e, cols, :]).astype(bf16)

    def unit_out(e):
        @pl.loop(0, 2)
        def _(c):
            cols = pl.ds(pl.multiple_of(c * 512, 512), 512)
            outp[e, :, cols] = mm(hid[e], wbk[e, :, cols]).astype(bf16)

    def scatter(part, bufs, e, at):
        rel, tot, arr = bufs
        return ReduceScatter(
            ring_x, part.at[e], Q, rel.at[e], tot.at[e], arr.at[e], rss.at[at]
        )

    rs_e = [scatter(n2p, (e_rel, e_sum, e_arr), e, 1 + e) for e in range(2)]
    rs_o = [scatter(outp, (o_rel, o_sum, o_arr), e, 3 + e) for e in range(2)]

    ag_x[0].wait_rest()
    unit(0)
    ag_x[1].pass_on()
    unit_n2(0)
    rs_e[0].send_all()
    unit_out(0)
    ag_x[1].wait_rest()
    unit(1)
    rs_e[0].pass_on()
    unit_n2(1)
    rs_e[1].send_all()
    unit_out(1)

    outs = [(xall, x_out), (gal, g_out), (hid, hid_out), (dpre, dpre_out)]
    stores = [pltpu.make_async_copy(a, b, loc.at[6 + i]) for i, (a, b) in enumerate(outs)]
    for copy in stores:
        copy.start()

    def send_back(rs, e, buf, x):
        value = rs.value().astype(bf16)
        for c in range(4):
            chunk = rem4(me // 8 + c)
            row0 = pl.multiple_of(chunk * 128, 128)
            r = iota((128, Q), 0) + row0
            sel = hot((r >> 4) * 4 + (r & 3) == iota((128, Q), 1))
            buf[e, pl.ds(row0, 128), :] = pick_quarter(mm(sel, value))
            x[e].start_chunk(chunk)
        x[e].keep_own()

    def to_tokens(buf, e):
        slots = slot_c[...]
        target = jnp.where(((slots >> 2) & 1) == e, (slots >> 3) * 16 + (slots & 3), -T)
        lanes = iota((Q, T), 1)
        return jnp.concatenate(
            [mm(hot(lanes == target + cq * 4), buf[e]) for cq in range(4)], axis=1
        )

    e_x = exchange(esend, erecv, es)
    o_x = exchange(osend, orecv, os_)

    rs_e[0].wait()
    send_back(rs_e[0], 0, esend, e_x)
    rs_e[1].pass_on()
    rs_o[0].send_all()
    rs_e[1].wait()
    send_back(rs_e[1], 1, esend, e_x)

    sel_own = hot(iota((Q, T), 0) + h * Q == iota((Q, T), 1))
    cot_q = mm(mm(sel_own, pm[...]).astype(bf16), cot_low[...])
    e_x[0].all.wait_recv()
    dn2 = to_tokens(erecv, 0)
    rs_o[0].pass_on()
    e_x[1].all.wait_recv()
    dn2 = dn2 + to_tokens(erecv, 1)
    xhat2, r2 = resid_norm()
    nv[2] = as_tile(jnp.sum(dn2 * xhat2, axis=0, keepdims=True))
    nv[3] = as_tile(jnp.sum(dn2, axis=0, keepdims=True))
    d_resid = cot_q + norm_back(dn2 * g2_ref[...], xhat2, r2)
    dres[...] = d_resid
    datt[own_rows, :] = d_resid.astype(bf16)
    ag_d = Gather(ring_x, datt, Q, ags.at[2])
    ag_d.start()
    ag_d.pass_on()
    rs_o[1].send_all()
    ag_d.wait_rest()

    stores[1].wait()
    dmx[...] = mm_nt(datt[...], wout[...]).astype(bf16)
    dm_t[...] = dmx[...].astype(f32).T.astype(bf16)

    @pl.loop(0, 4)
    def _(c):
        cols = pl.ds(pl.multiple_of(c * 256, 256), 256)
        rows = pl.ds(pl.multiple_of(lax.rem(c, 2) * 256, 256), 256)
        wpart[c // 2, rows, 768:1024] = mm(mixed_t[...], datt[:, cols]).astype(bf16)

    for hp in range(2):
        pair = slice(hp * 128, hp * 128 + 128)

        @pl.loop(0, 4)
        def _(rb):
            rows = pl.ds(pl.multiple_of(rb * Q, Q), Q)
            dqs = []
            for hh in range(2):
                lanes = slice(hp * 128 + hh * 64, hp * 128 + hh * 64 + 64)
                dch = mm_nt(dmx[rows, lanes], qkv[2, :, lanes])
                ch = chs[hp * 2 + hh, rows, :].astype(f32)
                inner = jnp.sum(ch * dch, axis=-1, keepdims=True)
                ds = (ch * (dch - inner)).astype(bf16)
                dss[hh][rows, :] = ds
                dqs.append(mm(ds, qkv[1, :, lanes]) * 0.125)
            dqkv[0, rows, pair] = jnp.concatenate(dqs, axis=1).astype(bf16)

        if hp == 0:
            rs_o[1].pass_on()
            rs_o[0].wait()
            send_back(rs_o[0], 0, osend, o_x)
        dks, dvs = [], []
        for hh in range(2):
            lanes = slice(hp * 128 + hh * 64, hp * 128 + hh * 64 + 64)
            dks.append(mm(q_t[lanes, :], dss[hh][...]) * 0.125)
            dvs.append(mm(dm_t[lanes, :], chs[hp * 2 + hh]))
        dqkv[1, :, pair] = jnp.concatenate(dks, axis=0).T.astype(bf16)
        dqkv[2, :, pair] = jnp.concatenate(dvs, axis=0).T.astype(bf16)

    rs_d = ReduceScatter(ring_x, npart, Q, d_rel, d_sum, d_arr, rss.at[5])

    def input_grad(b):
        rows = pl.ds(pl.multiple_of(b * Q, Q), Q)
        total = mm_nt(dqkv[0, rows, :], wqkv[0])
        for c in (1, 2):
            total += mm_nt(dqkv[c, rows, :], wqkv[c])
        npart[rows, :] = total.astype(bf16)

    input_grad(far)
    for copy in rs_d.far:
        copy.start()
    input_grad(left)
    rs_d.near[0].start()
    input_grad(right)
    rs_d.near[1].start()
    input_grad(h)

    for c in range(3):
        for k in range(2):
            rows = normed_t[k * T : (k + 1) * T, :]
            wpart[k, :, c * 256 : (c + 1) * 256] = mm(rows, dqkv[c]).astype(bf16)

    core_rows = pl.ds(pl.multiple_of(core * T, T), T)
    other_rows = pl.ds(pl.multiple_of((1 - core) * T, T), T)
    swap = remote(wpart.at[1 - core], wx, xs.at[0], xs.at[1], sibling)
    swap.start()
    rs_d.pass_on()
    rs_o[1].wait()
    send_back(rs_o[1], 1, osend, o_x)
    swap.wait_recv()
    ws[...] = (wpart[core].astype(f32) + wx[...].astype(f32)).astype(bf16)
    ws0, ws1 = ws.at[pl.ds(0, 256), :], ws.at[pl.ds(256, 256), :]

    def reduce(ring, part, rows, rel, tot, arr, at):
        return ReduceScatter(ring, part, rows, rel, tot, arr, rss.at[at])

    rs_w0 = reduce(ring_y, ws0, 64, w0_rel, w0_sum, w0_arr, 6)
    rs_w1 = reduce(ring_z, ws1, 64, w1_rel, w1_sum, w1_arr, 7)
    rs_w2 = reduce(ring_z, w0, 16, w2_rel, w2_sum, w2_arr, 8)
    rs_w3 = reduce(ring_y, w1, 16, w3_rel, w3_sum, w3_arr, 9)
    rs_w0.send_all()
    rs_w1.send_all()

    rs_d.wait()
    dn1 = rs_d.value()
    xhat1, r1 = norm_parts(xp[own_rows, :].astype(f32))
    gtall[own_rows, :] = (dres[...] + norm_back(dn1 * g1_ref[...], xhat1, r1)).astype(bf16)
    ag_g = Gather(ring_x, gtall, Q, ags.at[3])
    ag_g.start()
    nv[0] = as_tile(jnp.sum(dn1 * xhat1, axis=0, keepdims=True))
    nv[1] = as_tile(jnp.sum(dn1, axis=0, keepdims=True))

    def to_x(src, dst, mine, at):
        copies = [
            remote(src(rem4(h + k)), dst.at[mine], vs.at[at], vs.at[at + 1], {"head": rem4(h + k)})
            for k in (1, 2, 3)
        ]
        three = dst.at[pl.ds(0, 3)]
        for copy in copies:
            copy.start()
        return remote(three, three, vs.at[at], vs.at[at + 1], {"head": rem4(h + 1)})

    nx = to_x(lambda k: nv.at[k], nrx, h, 0)

    rs_w0.pass_on()
    rs_w1.pass_on()
    rs_w0.wait()
    w0[...] = rs_w0.value().astype(bf16)
    rs_w2.send_all()
    rs_w1.wait()
    w1[...] = rs_w1.value().astype(bf16)
    rs_w3.send_all()

    for e in range(2):
        o_x[e].all.wait_recv()
    outall[own_rows, :] = (att_q[...] + to_tokens(orecv, 0) + to_tokens(orecv, 1)).astype(bf16)
    ag_o = Gather(ring_x, outall, Q, ags.at[4])
    ag_g.pass_on()
    ag_o.start()
    rs_w2.pass_on()
    rs_w3.pass_on()

    nx.wait_recv()
    nye[me] = nv[h] + nrx[rem4(h + 1)] + nrx[rem4(h + 2)] + nrx[rem4(h + 3)]

    def n_all(d):
        return remote(nye.at[me], nye.at[me], vs.at[2], vs.at[3], {"expert": d})

    n_rows = nye.at[pl.ds(0, G - 1)]
    n_every = remote(n_rows, n_rows, vs.at[2], vs.at[3], {"expert": lax.rem(me + 1, G)})

    base = core * T
    row_y = pl.multiple_of(base + y * 64, 64)
    row_z = pl.multiple_of(base + 256 + z * 64, 64)

    def spread(ring, row0, rows, at):
        view = w_out.at[pl.ds(pl.multiple_of(row0, rows), 4 * rows), :]
        return Gather(ring, view, rows, ags.at[at])

    ag_w2 = spread(ring_z, row_y, 16, 5)
    ag_w3 = spread(ring_y, row_z, 16, 6)
    ag_w0 = spread(ring_y, base, 64, 7)
    ag_w1 = spread(ring_z, base + 256, 64, 8)
    rs_w2.wait()
    w_out[pl.ds(pl.multiple_of(row_y + z * 16, 16), 16), :] = rs_w2.value().astype(bf16)
    ag_w2.start()
    rs_w3.wait()
    w_out[pl.ds(pl.multiple_of(row_z + y * 16, 16), 16), :] = rs_w3.value().astype(bf16)
    ag_w3.start()
    others(lambda d: n_all(d).start())
    ag_w2.finish()
    ag_w0.start()
    ag_w3.finish()
    ag_w1.start()

    def restore(dst, src):
        @pl.loop(0, 4)
        def _(c):
            cols = pl.ds(pl.multiple_of(c * 256, 256), 256)
            dst[:, cols] = mm(pmt[...], src[:, cols]).astype(bf16)

    ag_o.pass_on()
    ag_w0.pass_on()
    ag_w1.pass_on()
    ag_g.wait_rest()
    restore(xp, gtall)
    gt_store = pltpu.make_async_copy(xp, gt_out, loc.at[10])
    gt_store.start()

    n_every.wait_recv()
    nrm_out[h] = jnp.sum(nye[...], axis=0)
    nf = to_x(lambda k: nrm_out.at[h], nrm_out, h, 4)

    ag_w0.wait_rest()
    ag_w1.wait_rest()
    both = remote(w_out.at[core_rows, :], w_out.at[core_rows, :], xs.at[2], xs.at[3], sibling)
    both_in = remote(w_out.at[core_rows, :], w_out.at[other_rows, :], xs.at[2], xs.at[3], sibling)
    both.start()
    ag_o.wait_rest()
    restore(normed, outall)
    u_store = pltpu.make_async_copy(normed, u_out, loc.at[11])
    u_store.start()
    both_in.wait_recv()
    nf.wait_recv()

    for x in n_x + e_x + o_x:
        x.all.wait_send()
    n_every.wait_send()
    for group in (rs_a, *rs_e, *rs_o, rs_d, rs_w0, rs_w1, rs_w2, rs_w3,
                  *ag_x, ag_d, ag_o, ag_g, ag_w0, ag_w1, ag_w2, ag_w3):
        group.wait_sent()
    swap.wait_send()
    both.wait_send()
    nx.wait_send()
    nf.wait_send()
    for copy in [stores[0], *stores[2:], gt_store, u_store]:
        copy.wait()


def layer(seg, route, g1, b1, g2, b2, tok, wqkv, wout, win, wbk, cot):
    vmem = pl.BlockSpec(memory_space=pltpu.VMEM)
    hbm = pl.BlockSpec(memory_space=pl.ANY)
    V = pltpu.VMEM
    DMA = pltpu.SemaphoreType.DMA

    def rs_bufs(rows, cols):
        return [V((2, rows, cols), bf16), V((2, rows, cols), bf16), V((2, 2, rows, cols), bf16)]

    pair_bufs = [V((2, *buf.shape), bf16) for buf in rs_bufs(Q, HALF)]
    scratch = [
        V((T, D), bf16), V((3, D, 256), bf16), V((256, D), bf16), V((2, D, D), bf16),
        V((2, D, D), bf16), V((T, D), f32), V((T, D), bf16),
        V((T, T), bf16), V((T, T), bf16), V((T, 1), i32), V((1, T), i32), V((Q, 1), i32),
        V((1, Q), i32),
        V((2, T, D), bf16), V((2, T, D), bf16), V((2, T, D), bf16),
        V((T, D), bf16), V((T, D), bf16), V((D, T), bf16), V((3, T, 256), bf16),
        V((256, T), bf16), V((4, T, T), bf16), V((T, 256), bf16), V((256, T), bf16),
        V((T, D), bf16), *rs_bufs(Q, HALF),
        V((Q, D), bf16), V((2, T, 256), bf16), V((2, T, 256), bf16), *[V((2, T, D), bf16)] * 4,
        *pair_bufs, V((2, T, 256), bf16), V((2, T, 256), bf16),
        *pair_bufs, V((2, T, 256), bf16), V((2, T, 256), bf16), V((T, D), bf16),
        V((T, D), bf16), V((T, 256), bf16), V((256, T), bf16), V((3, T, 256), bf16),
        *rs_bufs(Q, HALF), V((T, D), bf16),
        V((T, D), bf16),
        V((64, D), bf16), *rs_bufs(64, HALF), V((64, D), bf16), *rs_bufs(64, HALF),
        *rs_bufs(16, HALF), *rs_bufs(16, HALF),
        V((4, 8, 128), f32), V((4, 8, 128), f32), V((G, 8, 128), f32),
        DMA((12,)), DMA((2,)), *[DMA((2, 2))] * 3, DMA((10, 4)), DMA((9, 4)), DMA((4,)), DMA((6,)),
    ]
    S = jax.ShapeDtypeStruct
    quarters = S((2, T, D), bf16)
    return pl.pallas_call(
        layer_kernel,
        name="layer",
        out_shape=[quarters] * 4
        + [S((T, D), bf16), S((T, D), bf16), S((D, D), bf16), S((4, 8, 128), f32)],
        in_specs=[vmem] * 6 + [hbm] * 6,
        out_specs=[hbm] * 6 + [vmem] * 2,
        scratch_shapes=scratch,
        compiler_params=pltpu.CompilerParams(
            collective_id=0, has_side_effects=True, vmem_limit_bytes=62 << 20
        ),
        cost_estimate=pl.CostEstimate(
            flops=24 * 10**9, bytes_accessed=30 * 2**20, transcendentals=4 * 10**6
        ),
    )(seg, route, g1, b1, g2, b2, tok, wqkv, wout, win, wbk, cot)


def finish_kernel(
    x_ref, dpre_ref, hid_ref, g_ref, w_ref, u_ref, gt_ref, tok_ref,
    win_out, wback_out, wqkv_out, wout_out, out_out, gt_out,
):
    def outer(lhs, rhs, out):
        out[0] = lax.dot_general(
            lhs[0], rhs[0], (((0,), (0,)), ((), ())), preferred_element_type=f32
        )

    outer(x_ref, dpre_ref, win_out)
    outer(hid_ref, g_ref, wback_out)
    for c in range(3):
        wqkv_out[c] = w_ref[:, c * 256 : (c + 1) * 256].astype(f32)
    wout_out[...] = w_ref[:, 768:].astype(f32)
    out_out[...] = tok_ref[...].astype(f32) + u_ref[...].astype(f32)
    gt_out[...] = gt_ref[...].astype(f32)


def finish(x, dpre, hid, g, w, u, gt, tokens):
    lhs = pl.BlockSpec((1, T, 256), lambda e, c: (e, 0, c))
    rhs = pl.BlockSpec((1, T, D), lambda e, c: (e, 0, 0))
    out = pl.BlockSpec((1, 256, D), lambda e, c: (e, c, 0))
    rows = pl.BlockSpec((64, D), lambda e, c: (e * 4 + c, 0))
    S = jax.ShapeDtypeStruct
    return pl.pallas_call(
        finish_kernel,
        name="finish",
        grid=(2, 4),
        out_shape=[
            S((2, D, D), f32), S((2, D, D), f32), S((3, D, 256), f32), S((256, D), f32),
            S((T, D), f32), S((T, D), f32),
        ],
        in_specs=[lhs, rhs, lhs, rhs, pl.BlockSpec((128, D), lambda e, c: (e * 4 + c, 0)),
                  rows, rows, rows],
        out_specs=[
            out, out,
            pl.BlockSpec((3, 128, 256), lambda e, c: (0, e * 4 + c, 0)),
            pl.BlockSpec((128, 256), lambda e, c: (c % 2, e * 2 + c // 2)),
            rows, rows,
        ],
        compiler_params=pltpu.CompilerParams(vmem_limit_bytes=60 << 20),
        cost_estimate=pl.CostEstimate(
            flops=8 * 2**30, bytes_accessed=37 * 2**20, transcendentals=0
        ),
    )(x, dpre, hid, g, w, u, gt, tokens)


def per_device(
    tokens, segment_ids, expert_of, norm1_gain, norm1_bias, norm2_gain, norm2_bias,
    w_qkv, w_out, w_in, w_back, cotangent,
):
    row = lambda v: v.reshape(1, D)
    x, g, hid, dpre, u, gt, w, nrm = layer(
        segment_ids, expert_of.reshape(1, T), row(norm1_gain), row(norm1_bias), row(norm2_gain), row(norm2_bias),
        tokens, w_qkv, w_out, w_in, w_back, cotangent,
    )
    grad_w_in, grad_w_back, grad_w_qkv, grad_w_out, output, grad_tokens = finish(
        x, dpre, hid, g, w, u, gt, tokens
    )
    vectors = nrm.reshape(4, D)
    return (
        output, grad_tokens, vectors[0], vectors[1], vectors[2], vectors[3],
        grad_w_qkv, grad_w_out, grad_w_in, grad_w_back,
    )


def solution(mesh):
    return jax.shard_map(
        per_device,
        mesh=mesh,
        in_specs=(
            P("expert", None),
            P("expert", None),
            P("expert", None),
            P(),
            P(),
            P(),
            P(),
            P(None, None, "head"),
            P("head", None),
            P("expert", None, "head"),
            P("expert", "head", None),
            P("expert", None),
        ),
        out_specs=(
            P("expert", None),
            P("expert", None),
            P(),
            P(),
            P(),
            P(),
            P(None, None, "head"),
            P("head", None),
            P("expert", None, "head"),
            P("expert", "head", None),
        ),
        check_vma=False,
    )
```

time: 224 us -> 180 us (0.80)
  Pallas kernels: 202 us -> 178 us
  local copies, waits for them, and re-layouts: 17.5 us -> 1.3 us
  other arithmetic: 3.27 us -> 0 us
    pallas_call x1, Pallas kernels: 193 us -> 162 us  [layer(): pl.pallas_call(layer_kernel, name='layer', out_shape=[quarters] * 4 + [S(...]
    unnamed x20 -> x0, local copies, waits for them, and re-layouts: 10.3 us -> none
    pallas_call x1, Pallas kernels: 8.65 us -> 16 us  [finish(): pl.pallas_call(finish_kernel, name='finish', grid=(2, 4), out_shape=[S((2...]
    slice x3 -> x0, local copies, waits for them, and re-layouts: 5.55 us -> none  [the longest x2 4.29 us: per_device(): grad_w_qkv = jnp.moveaxis(w[:, :768].reshape(D, 3, 256), 1, 0)]
where the time goes in v2:
time: 180 us
  Pallas kernels  178 us (99%)
    pallas_call x1, Pallas kernels, layer(): pl.pallas_call(layer_kernel, name='layer', out_shape=[quarters] * 4 + [S(...  162 us
    pallas_call x1, Pallas kernels, finish(): pl.pallas_call(finish_kernel, name='finish', grid=(2, 4), out_shape=[S((2...  16 us

profile of v2, /device:TPU:1, one launch (start us, length us, event | category | flops | bytes accessed | tf_op | source)
XLA Modules:
  0.0 179.9 jit_solution(10620059652565592227)
XLA Ops:
  0.6 161.8 %layer.1 = (bf16[2,512,1024]{2,1,0:T(8,128)(2,1)}, bf16[2,512,1024]{2,1,0:T(8,128)(2,1)}, bf16[2,512,1024]{2,1,0:T(8,128)(2,1)}, bf16[2,512,1024]{2,1,0:T(8,128)...) custom-call(s32[1,512]{1,0:T(1,128)} %seg_ref.1, ...), custom_call_target="tpu_custom_call" | custom-call | flops 24000000000 | bytes 31457280 | tf_op jit(solution)/shard_map/layer/pallas_call | solution.py:779
  162.4 1.3 slice_bitcast_fusion
  163.7 16.0 %finish.1 = (f32[2,1024,1024]{2,1,0:T(8,128)}, f32[2,1024,1024]{2,1,0:T(8,128)}, f32[3,1024,256]{2,1,0:T(8,128)}, f32[256,1024]{1,0:T(8,128)}, f32[512,1024]{1,0:T(8,128)}, /*index=5*/f32[512,1024]{1,0:T(8,128)}) custom-call(bf16[2,512,1024]{2,1,0:T(8,128)(2,1)} %get-tuple-element.24.x_ref, bf16[2,512,1024]{2,1,0:T(8,128)(2,1)} %get-tuple-element.25.dpre_ref, ...), custom_call_target="tpu_custom_call" | custom-call | flops 8589934592 | bytes 38797312 | tf_op jit(solution)/shard_map/finish/pallas_call | solution.py:820

commit v3 on v2

--- a/solution.py
+++ b/solution.py
@@ -200,18 +200,18 @@
 def layer_kernel(
     seg_ref, route_ref, g1_ref, b1_ref, g2_ref, b2_ref,
     tok_hbm, wqkv_hbm, wout_hbm, win_hbm, wbk_hbm, cot_hbm,
-    x_out, g_out, hid_out, dpre_out, u_out, gt_out, w_out, nrm_out,
+    x_out, g_out, hid_out, dpre_out, u_out, gt_out, pmt_out, w_out, nrm_out,
     tok, wqkv, wout, win, wbk, cotw, cot_low,
     pm, pmt, code_c, code_r, slot_c, slot_r,
     csend, crecv, gal,
-    xp, normed, normed_t, qkv, q_t, chs, mixed, mixed_t,
+    xp, normed, normed_t, qkv, k_t, chs, mixed, mixed_t,
     apart, a_rel, a_sum, a_arr,
     norm2, nsend, nrecv, xall, hid, dpre, n2p,
     e_rel, e_sum, e_arr, esend, erecv,
     o_rel, o_sum, o_arr, osend, orecv, outall,
-    datt, dmx, dm_t, dqkv,
+    datt, dmx, v_t, dqkv,
     d_rel, d_sum, d_arr, gtall,
-    wx,
+    wx, wfin,
     w0, w0_rel, w0_sum, w0_arr, w1, w1_rel, w1_sum, w1_arr,
     w2_rel, w2_sum, w2_arr, w3_rel, w3_sum, w3_arr,
     nv, nrx, nye,
@@ -233,11 +233,11 @@
     sibling = {"expert": chip * 2 + 1 - core}
     left, right, far = rem4(h + 3), rem4(h + 1), rem4(h + 2)
 
-    att_q, dres = cotw.at[pl.ds(0, Q), :], cotw.at[pl.ds(Q, Q), :]
+    att_q, dres, cot_q = (cotw.at[pl.ds(k * Q, Q), :] for k in range(3))
     npart = tok
     ws = cot_low
     wpart = gal
-    dss = [tok.at[:, pl.ds(0, T)], tok.at[:, pl.ds(T, T)]]
+    dss = [buf.at[:, pl.ds(k * T, T)] for buf in (tok, apart) for k in range(2)]
     outp = csend
 
     loads = {}
@@ -312,7 +312,14 @@
     def exchange(src, dst, sems):
         return [Exchange(me, src.at[e], dst.at[e], sems.at[e]) for e in range(2)]
 
-    cot_x = Exchange(me, csend, crecv, cs)
+    cot_x = exchange(csend, crecv, cs)
+
+    def send_cot(e):
+        @pl.loop(0, 4)
+        def _(c):
+            cot_x[e].start_chunk(rem4(me // 8 + c))
+
+        cot_x[e].keep_own()
 
     @pl.loop(0, 4)
     def _(c):
@@ -323,9 +330,9 @@
         rows = mm(sel, cot_low[...]).astype(bf16)
         for e in range(2):
             csend[e, pl.ds(row0, 128), :] = rows[e * 128 : e * 128 + 128]
-        cot_x.start_chunk(chunk)
-
-    cot_x.keep_own()
+        cot_x[0].start_chunk(chunk)
+
+    cot_x[0].keep_own()
 
     loads["tok"].wait()
 
@@ -341,27 +348,29 @@
 
     @pl.loop(0, 3)
     def _(c):
-        qkv[c] = mm(normed[...], wqkv[c]).astype(bf16)
-
-    for hp in range(2):
-        pair = slice(hp * 128, hp * 128 + 128)
-
-        @pl.loop(0, 4)
-        def _(rb):
-            rows = pl.ds(pl.multiple_of(rb * Q, Q), Q)
-            codes = code_c[rows, :]
-            keys = code_r[...]
-            allowed = (keys <= codes) & (keys >= ((codes >> 10) << 10))
-            outs = []
-            for hh in range(2):
-                lanes = slice(hp * 128 + hh * 64, hp * 128 + hh * 64 + 64)
-                s = mm_nt(qkv[0, rows, lanes], qkv[1, :, lanes]) * 0.125
-                s = jnp.where(allowed, s, -1e30)
-                e = jnp.exp(s - jnp.max(s, axis=-1, keepdims=True))
-                ch = (e * (1.0 / jnp.sum(e, axis=-1, keepdims=True))).astype(bf16)
-                chs[hp * 2 + hh, rows, :] = ch
-                outs.append(mm(ch, qkv[2, :, lanes]))
-            mixed[rows, pair] = jnp.concatenate(outs, axis=1).astype(bf16)
+        qkv[c] = (mm(normed[...], wqkv[c]) * jnp.where(c == 0, 0.125, 1.0)).astype(bf16)
+
+    v_t[...] = qkv[2].astype(f32).T.astype(bf16)
+
+    def head(hd):
+        return slice(hd * 64, hd * 64 + 64)
+
+    @pl.loop(0, 4)
+    def _(rb):
+        rows = pl.ds(pl.multiple_of(rb * Q, Q), Q)
+        keys, queries = code_c[...], code_r[:, rows]
+        allowed = (keys <= queries) & (keys >= ((queries >> 10) << 10))
+        bias = jnp.where(allowed, 0.0, -1e30)
+        outs = []
+        for hd in range(4):
+            s = mm_nt(qkv[1, :, head(hd)], qkv[0, rows, head(hd)]) + bias
+            e = jnp.exp(s - jnp.max(s, axis=0, keepdims=True))
+            ch = (e * (1.0 / jnp.sum(e, axis=0, keepdims=True))).astype(bf16)
+            chs[hd, :, rows] = ch
+            outs.append(mm(v_t[head(hd), :], ch))
+        heads = jnp.concatenate(outs, axis=0)
+        mixed_t[:, rows] = heads.astype(bf16)
+        mixed[rows, :] = heads.T.astype(bf16)
 
     loads["wout"].wait()
     rs_a = ReduceScatter(ring_x, apart, Q, a_rel, a_sum, a_arr, rss.at[0])
@@ -381,8 +390,7 @@
     own_rows = pl.ds(pl.multiple_of(h * Q, Q), Q)
 
     rs_a.pass_on()
-    q_t[...] = qkv[0].astype(f32).T.astype(bf16)
-    mixed_t[...] = mixed[...].astype(f32).T.astype(bf16)
+    k_t[...] = qkv[1].astype(f32).T.astype(bf16)
 
     @pl.loop(0, 4)
     def _(c):
@@ -419,17 +427,20 @@
 
         n_x[e].keep_own()
 
-    cot_x.all.wait_recv()
-
+    sel_own = hot(iota((Q, T), 0) + h * Q == iota((Q, T), 1))
+    cot_q[...] = mm(mm(sel_own, pm[...]).astype(bf16), cot_low[...])
     i = iota((T, T), 0)
-    reorder = hot(((i & 127) >> 2) * 16 + (i >> 7) * 4 + (i & 3) == iota((T, T), 1))
-    for e in range(2):
+    pm[...] = hot(((i & 127) >> 2) * 16 + (i >> 7) * 4 + (i & 3) == iota((T, T), 1))
+
+    def regroup(e):
+        cot_x[e].all.wait_recv()
 
         @pl.loop(0, 4)
         def _(c):
             cols = pl.ds(pl.multiple_of(c * 256, 256), 256)
-            gal[e, :, cols] = mm(reorder, crecv[e, :, cols]).astype(bf16)
-
+            gal[e, :, cols] = mm(pm[...], crecv[e, :, cols]).astype(bf16)
+
+    regroup(0)
     ag_x = [Gather(ring_x, xall.at[e], Q, ags.at[e]) for e in range(2)]
 
     def compact(e):
@@ -443,12 +454,12 @@
     compact(0)
     ag_x[0].start()
     compact(1)
+    send_cot(1)
     ag_x[0].pass_on()
     ag_x[1].start()
 
     loads["win"].wait()
     loads["wbk"].wait()
-    cot_x.all.wait_send()
 
     def unit(e):
         @pl.loop(0, 2)
@@ -484,7 +495,10 @@
     ag_x[1].pass_on()
     unit_n2(0)
     rs_e[0].send_all()
+    for x in cot_x:
+        x.all.wait_send()
     unit_out(0)
+    regroup(1)
     ag_x[1].wait_rest()
     unit(1)
     rs_e[0].pass_on()
@@ -492,7 +506,7 @@
     rs_e[1].send_all()
     unit_out(1)
 
-    outs = [(xall, x_out), (gal, g_out), (hid, hid_out), (dpre, dpre_out)]
+    outs = [(xall, x_out), (gal, g_out), (hid, hid_out), (dpre, dpre_out), (pmt, pmt_out)]
     stores = [pltpu.make_async_copy(a, b, loc.at[6 + i]) for i, (a, b) in enumerate(outs)]
     for copy in stores:
         copy.start()
@@ -526,8 +540,6 @@
     rs_e[1].wait()
     send_back(rs_e[1], 1, esend, e_x)
 
-    sel_own = hot(iota((Q, T), 0) + h * Q == iota((Q, T), 1))
-    cot_q = mm(mm(sel_own, pm[...]).astype(bf16), cot_low[...])
     e_x[0].all.wait_recv()
     dn2 = to_tokens(erecv, 0)
     rs_o[0].pass_on()
@@ -536,7 +548,7 @@
     xhat2, r2 = resid_norm()
     nv[2] = as_tile(jnp.sum(dn2 * xhat2, axis=0, keepdims=True))
     nv[3] = as_tile(jnp.sum(dn2, axis=0, keepdims=True))
-    d_resid = cot_q + norm_back(dn2 * g2_ref[...], xhat2, r2)
+    d_resid = cot_q[...] + norm_back(dn2 * g2_ref[...], xhat2, r2)
     dres[...] = d_resid
     datt[own_rows, :] = d_resid.astype(bf16)
     ag_d = Gather(ring_x, datt, Q, ags.at[2])
@@ -547,42 +559,147 @@
 
     stores[1].wait()
     dmx[...] = mm_nt(datt[...], wout[...]).astype(bf16)
-    dm_t[...] = dmx[...].astype(f32).T.astype(bf16)
-
-    @pl.loop(0, 4)
-    def _(c):
-        cols = pl.ds(pl.multiple_of(c * 256, 256), 256)
-        rows = pl.ds(pl.multiple_of(lax.rem(c, 2) * 256, 256), 256)
-        wpart[c // 2, rows, 768:1024] = mm(mixed_t[...], datt[:, cols]).astype(bf16)
-
     for hp in range(2):
         pair = slice(hp * 128, hp * 128 + 128)
-
-        @pl.loop(0, 4)
-        def _(rb):
-            rows = pl.ds(pl.multiple_of(rb * Q, Q), Q)
-            dqs = []
-            for hh in range(2):
-                lanes = slice(hp * 128 + hh * 64, hp * 128 + hh * 64 + 64)
-                dch = mm_nt(dmx[rows, lanes], qkv[2, :, lanes])
-                ch = chs[hp * 2 + hh, rows, :].astype(f32)
-                inner = jnp.sum(ch * dch, axis=-1, keepdims=True)
-                ds = (ch * (dch - inner)).astype(bf16)
-                dss[hh][rows, :] = ds
-                dqs.append(mm(ds, qkv[1, :, lanes]) * 0.125)
-            dqkv[0, rows, pair] = jnp.concatenate(dqs, axis=1).astype(bf16)
-
-        if hp == 0:
-            rs_o[1].pass_on()
-            rs_o[0].wait()
-            send_back(rs_o[0], 0, osend, o_x)
-        dks, dvs = [], []
-        for hh in range(2):
-            lanes = slice(hp * 128 + hh * 64, hp * 128 + hh * 64 + 64)
-            dks.append(mm(q_t[lanes, :], dss[hh][...]) * 0.125)
-            dvs.append(mm(dm_t[lanes, :], chs[hp * 2 + hh]))
-        dqkv[1, :, pair] = jnp.concatenate(dks, axis=0).T.astype(bf16)
-        dqkv[2, :, pair] = jnp.concatenate(dvs, axis=0).T.astype(bf16)
+        dvs = [mm(chs[hd], dmx[:, head(hd)]) for hd in (2 * hp, 2 * hp + 1)]
+        dqkv[2, :, pair] = jnp.concatenate(dvs, axis=1).astype(bf16)
+
+    def weight_part(c, lanes):
+        for k in range(2):
+            rows = normed_t[k * T : (k + 1) * T, :]
+            wpart[k, :, lanes] = mm(rows, dqkv[c]).astype(bf16)
+
+    for k in range(4):
+        block = mm(mixed_t[...], datt[:, k * 256 : (k + 1) * 256]).astype(bf16)
+        wpart[k // 2, (k % 2) * 256 : (k % 2) * 256 + 256, 0:256] = block
+    weight_part(2, slice(256, 512))
+
+    class WeightSum:
+        def __init__(self, k):
+            cols, thin = pl.ds(k * T, T), pl.ds(k * 256, 256)
+            both = pl.ds(0, 2)
+            core_rows = pl.ds(pl.multiple_of(core * T, T), T)
+            other_rows = pl.ds(pl.multiple_of((1 - core) * T, T), T)
+            base = core * T
+            self.mine, self.got, self.ws = wpart.at[core, :, cols], wx.at[:, cols], ws.at[:, cols]
+            self.w0, self.w1 = w0.at[:, cols], w1.at[:, cols]
+            sem = xs.at[k]
+            self.swap = remote(
+                wpart.at[1 - core, :, cols], self.got, sem.at[0], sem.at[1], sibling
+            )
+
+            def scatter(ring, part, rows, bufs, at):
+                rel, tot, arr = bufs
+                return ReduceScatter(
+                    ring, part, rows, rel.at[both, :, thin], tot.at[both, :, thin],
+                    arr.at[both, both, :, thin], rss.at[6 + 4 * k + at],
+                )
+
+            def spread(ring, row0, rows, at):
+                view = wfin.at[pl.ds(pl.multiple_of(row0, rows), 4 * rows), cols]
+                return Gather(ring, view, rows, ags.at[5 + 4 * k + at])
+
+            self.rs0 = scatter(ring_y, ws.at[pl.ds(0, 256), cols], 64, (w0_rel, w0_sum, w0_arr), 0)
+            self.rs1 = scatter(ring_z, ws.at[pl.ds(256, 256), cols], 64, (w1_rel, w1_sum, w1_arr), 1)
+            self.rs2 = scatter(ring_z, self.w0, 16, (w2_rel, w2_sum, w2_arr), 2)
+            self.rs3 = scatter(ring_y, self.w1, 16, (w3_rel, w3_sum, w3_arr), 3)
+            row_y, row_z = base + y * 64, base + 256 + z * 64
+            self.last = [
+                wfin.at[pl.ds(pl.multiple_of(row_y + z * 16, 16), 16), cols],
+                wfin.at[pl.ds(pl.multiple_of(row_z + y * 16, 16), 16), cols],
+            ]
+            self.ag0, self.ag1 = spread(ring_y, base, 64, 0), spread(ring_z, base + 256, 64, 1)
+            self.ag2, self.ag3 = spread(ring_z, row_y, 16, 2), spread(ring_y, row_z, 16, 3)
+            done = wfin.at[core_rows, cols]
+            self.give = remote(done, done, sem.at[2], sem.at[3], sibling)
+            self.take = remote(done, wfin.at[other_rows, cols], sem.at[2], sem.at[3], sibling)
+            self.store = pltpu.make_async_copy(
+                wfin.at[:, cols], w_out.at[:, cols], loc.at[12 + k]
+            )
+
+        def step(self, n):
+            if n == 0:
+                self.swap.start()
+            elif n == 1:
+                self.swap.wait_recv()
+                self.ws[...] = (self.mine[...].astype(f32) + self.got[...].astype(f32)).astype(bf16)
+                self.rs0.send_all()
+                self.rs1.send_all()
+            elif n == 2:
+                self.rs0.pass_on()
+                self.rs1.pass_on()
+            elif n == 3:
+                self.rs0.wait()
+                self.w0[...] = self.rs0.value().astype(bf16)
+                self.rs2.send_all()
+                self.rs1.wait()
+                self.w1[...] = self.rs1.value().astype(bf16)
+                self.rs3.send_all()
+            elif n == 4:
+                self.rs2.pass_on()
+                self.rs3.pass_on()
+            elif n == 5:
+                self.rs2.wait()
+                self.last[0][...] = self.rs2.value().astype(bf16)
+                self.ag2.start()
+                self.rs3.wait()
+                self.last[1][...] = self.rs3.value().astype(bf16)
+                self.ag3.start()
+            elif n == 6:
+                self.ag2.pass_on()
+                self.ag3.pass_on()
+            elif n == 7:
+                self.ag2.wait_rest()
+                self.ag0.start()
+                self.ag3.wait_rest()
+                self.ag1.start()
+            elif n == 8:
+                self.ag0.pass_on()
+                self.ag1.pass_on()
+            elif n == 9:
+                self.ag0.wait_rest()
+                self.ag1.wait_rest()
+                self.give.start()
+            else:
+                self.take.wait_recv()
+                self.store.start()
+
+        def wait_sent(self):
+            self.swap.wait_send()
+            self.give.wait_send()
+            for group in (self.rs0, self.rs1, self.rs2, self.rs3,
+                          self.ag0, self.ag1, self.ag2, self.ag3):
+                group.wait_sent()
+            self.store.wait()
+
+    sum_a = WeightSum(0)
+    sum_a.step(0)
+    rs_a.wait_sent()
+
+    def backward(rb):
+        rows = pl.ds(pl.multiple_of(rb * Q, Q), Q)
+        dqs = []
+        for hd in range(4):
+            dch = mm_nt(qkv[2, :, head(hd)], dmx[rows, head(hd)])
+            ch = chs[hd, :, rows].astype(f32)
+            inner = jnp.sum(ch * dch, axis=0, keepdims=True)
+            ds = (ch * (dch - inner)).astype(bf16)
+            dss[hd][:, rows] = ds
+            dqs.append(mm(k_t[head(hd), :], ds) * 0.125)
+        dqkv[0, rows, :] = jnp.concatenate(dqs, axis=0).T.astype(bf16)
+
+    pl.loop(0, 2)(backward)
+    sum_a.step(1)
+    rs_o[1].pass_on()
+    pl.loop(2, 4)(backward)
+    sum_a.step(2)
+    rs_o[0].wait()
+    send_back(rs_o[0], 0, osend, o_x)
+    for hp in range(2):
+        pair = slice(hp * 128, hp * 128 + 128)
+        dks = [mm(dss[hd][...], qkv[0, :, head(hd)]) for hd in (2 * hp, 2 * hp + 1)]
+        dqkv[1, :, pair] = jnp.concatenate(dks, axis=1).astype(bf16)
+    sum_a.step(3)
 
     rs_d = ReduceScatter(ring_x, npart, Q, d_rel, d_sum, d_arr, rss.at[5])
 
@@ -602,35 +719,21 @@
     rs_d.near[1].start()
     input_grad(h)
 
-    for c in range(3):
-        for k in range(2):
-            rows = normed_t[k * T : (k + 1) * T, :]
-            wpart[k, :, c * 256 : (c + 1) * 256] = mm(rows, dqkv[c]).astype(bf16)
-
-    core_rows = pl.ds(pl.multiple_of(core * T, T), T)
-    other_rows = pl.ds(pl.multiple_of((1 - core) * T, T), T)
-    swap = remote(wpart.at[1 - core], wx, xs.at[0], xs.at[1], sibling)
-    swap.start()
+    weight_part(0, slice(512, 768))
+    weight_part(1, slice(768, 1024))
+    sum_b = WeightSum(1)
+    sum_b.step(0)
+    sum_a.step(4)
     rs_d.pass_on()
+    sum_a.step(5)
     rs_o[1].wait()
     send_back(rs_o[1], 1, osend, o_x)
-    swap.wait_recv()
-    ws[...] = (wpart[core].astype(f32) + wx[...].astype(f32)).astype(bf16)
-    ws0, ws1 = ws.at[pl.ds(0, 256), :], ws.at[pl.ds(256, 256), :]
-
-    def reduce(ring, part, rows, rel, tot, arr, at):
-        return ReduceScatter(ring, part, rows, rel, tot, arr, rss.at[at])
-
-    rs_w0 = reduce(ring_y, ws0, 64, w0_rel, w0_sum, w0_arr, 6)
-    rs_w1 = reduce(ring_z, ws1, 64, w1_rel, w1_sum, w1_arr, 7)
-    rs_w2 = reduce(ring_z, w0, 16, w2_rel, w2_sum, w2_arr, 8)
-    rs_w3 = reduce(ring_y, w1, 16, w3_rel, w3_sum, w3_arr, 9)
-    rs_w0.send_all()
-    rs_w1.send_all()
-
+    sum_b.step(1)
+    sum_a.step(6)
+
+    xhat1, r1 = norm_parts(xp[own_rows, :].astype(f32))
     rs_d.wait()
     dn1 = rs_d.value()
-    xhat1, r1 = norm_parts(xp[own_rows, :].astype(f32))
     gtall[own_rows, :] = (dres[...] + norm_back(dn1 * g1_ref[...], xhat1, r1)).astype(bf16)
     ag_g = Gather(ring_x, gtall, Q, ags.at[3])
     ag_g.start()
@@ -648,96 +751,52 @@
         return remote(three, three, vs.at[at], vs.at[at + 1], {"head": rem4(h + 1)})
 
     nx = to_x(lambda k: nv.at[k], nrx, h, 0)
-
-    rs_w0.pass_on()
-    rs_w1.pass_on()
-    rs_w0.wait()
-    w0[...] = rs_w0.value().astype(bf16)
-    rs_w2.send_all()
-    rs_w1.wait()
-    w1[...] = rs_w1.value().astype(bf16)
-    rs_w3.send_all()
+    sum_b.step(2)
+    sum_a.step(7)
+    sum_b.step(3)
+    nx.wait_recv()
+    nye[me] = nv[h] + nrx[rem4(h + 1)] + nrx[rem4(h + 2)] + nrx[rem4(h + 3)]
+
+    def n_all(d):
+        return remote(nye.at[me], nye.at[me], vs.at[2], vs.at[3], {"expert": d})
+
+    n_rows = nye.at[pl.ds(0, G - 1)]
+    n_every = remote(n_rows, n_rows, vs.at[2], vs.at[3], {"expert": lax.rem(me + 1, G)})
+    others(lambda d: n_all(d).start())
+    sum_a.step(8)
+    ag_g.pass_on()
+    sum_b.step(4)
 
     for e in range(2):
         o_x[e].all.wait_recv()
     outall[own_rows, :] = (att_q[...] + to_tokens(orecv, 0) + to_tokens(orecv, 1)).astype(bf16)
     ag_o = Gather(ring_x, outall, Q, ags.at[4])
-    ag_g.pass_on()
     ag_o.start()
-    rs_w2.pass_on()
-    rs_w3.pass_on()
-
-    nx.wait_recv()
-    nye[me] = nv[h] + nrx[rem4(h + 1)] + nrx[rem4(h + 2)] + nrx[rem4(h + 3)]
-
-    def n_all(d):
-        return remote(nye.at[me], nye.at[me], vs.at[2], vs.at[3], {"expert": d})
-
-    n_rows = nye.at[pl.ds(0, G - 1)]
-    n_every = remote(n_rows, n_rows, vs.at[2], vs.at[3], {"expert": lax.rem(me + 1, G)})
-
-    base = core * T
-    row_y = pl.multiple_of(base + y * 64, 64)
-    row_z = pl.multiple_of(base + 256 + z * 64, 64)
-
-    def spread(ring, row0, rows, at):
-        view = w_out.at[pl.ds(pl.multiple_of(row0, rows), 4 * rows), :]
-        return Gather(ring, view, rows, ags.at[at])
-
-    ag_w2 = spread(ring_z, row_y, 16, 5)
-    ag_w3 = spread(ring_y, row_z, 16, 6)
-    ag_w0 = spread(ring_y, base, 64, 7)
-    ag_w1 = spread(ring_z, base + 256, 64, 8)
-    rs_w2.wait()
-    w_out[pl.ds(pl.multiple_of(row_y + z * 16, 16), 16), :] = rs_w2.value().astype(bf16)
-    ag_w2.start()
-    rs_w3.wait()
-    w_out[pl.ds(pl.multiple_of(row_z + y * 16, 16), 16), :] = rs_w3.value().astype(bf16)
-    ag_w3.start()
-    others(lambda d: n_all(d).start())
-    ag_w2.finish()
-    ag_w0.start()
-    ag_w3.finish()
-    ag_w1.start()
-
-    def restore(dst, src):
-        @pl.loop(0, 4)
-        def _(c):
-            cols = pl.ds(pl.multiple_of(c * 256, 256), 256)
-            dst[:, cols] = mm(pmt[...], src[:, cols]).astype(bf16)
-
-    ag_o.pass_on()
-    ag_w0.pass_on()
-    ag_w1.pass_on()
-    ag_g.wait_rest()
-    restore(xp, gtall)
-    gt_store = pltpu.make_async_copy(xp, gt_out, loc.at[10])
-    gt_store.start()
-
+    sum_b.step(5)
+    sum_a.step(9)
+    sum_b.step(6)
     n_every.wait_recv()
     nrm_out[h] = jnp.sum(nye[...], axis=0)
     nf = to_x(lambda k: nrm_out.at[h], nrm_out, h, 4)
-
-    ag_w0.wait_rest()
-    ag_w1.wait_rest()
-    both = remote(w_out.at[core_rows, :], w_out.at[core_rows, :], xs.at[2], xs.at[3], sibling)
-    both_in = remote(w_out.at[core_rows, :], w_out.at[other_rows, :], xs.at[2], xs.at[3], sibling)
-    both.start()
+    sum_b.step(7)
+    sum_a.step(10)
+    ag_o.pass_on()
+    sum_b.step(8)
+    ag_g.wait_rest()
+    gt_store = pltpu.make_async_copy(gtall, gt_out, loc.at[14])
+    gt_store.start()
+    sum_b.step(9)
     ag_o.wait_rest()
-    restore(normed, outall)
-    u_store = pltpu.make_async_copy(normed, u_out, loc.at[11])
+    u_store = pltpu.make_async_copy(outall, u_out, loc.at[11])
     u_store.start()
-    both_in.wait_recv()
     nf.wait_recv()
+    sum_b.step(10)
 
     for x in n_x + e_x + o_x:
         x.all.wait_send()
     n_every.wait_send()
-    for group in (rs_a, *rs_e, *rs_o, rs_d, rs_w0, rs_w1, rs_w2, rs_w3,
-                  *ag_x, ag_d, ag_o, ag_g, ag_w0, ag_w1, ag_w2, ag_w3):
+    for group in (*rs_e, *rs_o, rs_d, *ag_x, ag_d, ag_o, ag_g, sum_a, sum_b):
         group.wait_sent()
-    swap.wait_send()
-    both.wait_send()
     nx.wait_send()
     nf.wait_send()
     for copy in [stores[0], *stores[2:], gt_store, u_store]:
@@ -768,11 +827,11 @@
         *pair_bufs, V((2, T, 256), bf16), V((2, T, 256), bf16), V((T, D), bf16),
         V((T, D), bf16), V((T, 256), bf16), V((256, T), bf16), V((3, T, 256), bf16),
         *rs_bufs(Q, HALF), V((T, D), bf16),
-        V((T, D), bf16),
+        V((T, D), bf16), V((D, D), bf16),
         V((64, D), bf16), *rs_bufs(64, HALF), V((64, D), bf16), *rs_bufs(64, HALF),
         *rs_bufs(16, HALF), *rs_bufs(16, HALF),
         V((4, 8, 128), f32), V((4, 8, 128), f32), V((G, 8, 128), f32),
-        DMA((12,)), DMA((2,)), *[DMA((2, 2))] * 3, DMA((10, 4)), DMA((9, 4)), DMA((4,)), DMA((6,)),
+        DMA((15,)), *[DMA((2, 2))] * 4, DMA((14, 4)), DMA((13, 4)), DMA((2, 4)), DMA((6,)),
     ]
     S = jax.ShapeDtypeStruct
     quarters = S((2, T, D), bf16)
@@ -780,9 +839,9 @@
         layer_kernel,
         name="layer",
         out_shape=[quarters] * 4
-        + [S((T, D), bf16), S((T, D), bf16), S((D, D), bf16), S((4, 8, 128), f32)],
+        + [S((T, D), bf16), S((T, D), bf16), S((T, T), bf16), S((D, D), bf16), S((4, 8, 128), f32)],
         in_specs=[vmem] * 6 + [hbm] * 6,
-        out_specs=[hbm] * 6 + [vmem] * 2,
+        out_specs=[hbm] * 8 + [vmem],
         scratch_shapes=scratch,
         compiler_params=pltpu.CompilerParams(
             collective_id=0, has_side_effects=True, vmem_limit_bytes=62 << 20
@@ -794,50 +853,86 @@
 
 
 def finish_kernel(
-    x_ref, dpre_ref, hid_ref, g_ref, w_ref, u_ref, gt_ref, tok_ref,
+    x_hbm, dpre_hbm, hid_hbm, g_hbm, w_hbm, u_hbm, gt_hbm, pmt_hbm, tok_hbm,
     win_out, wback_out, wqkv_out, wout_out, out_out, gt_out,
+    x, dpre, hid, g, w, u, gt, pmt, tok, win, wback, wqkv, wout, out, gtok, load, store,
 ):
-    def outer(lhs, rhs, out):
-        out[0] = lax.dot_general(
-            lhs[0], rhs[0], (((0,), (0,)), ((), ())), preferred_element_type=f32
-        )
-
-    outer(x_ref, dpre_ref, win_out)
-    outer(hid_ref, g_ref, wback_out)
-    for c in range(3):
-        wqkv_out[c] = w_ref[:, c * 256 : (c + 1) * 256].astype(f32)
-    wout_out[...] = w_ref[:, 768:].astype(f32)
-    out_out[...] = tok_ref[...].astype(f32) + u_ref[...].astype(f32)
-    gt_out[...] = gt_ref[...].astype(f32)
-
-
-def finish(x, dpre, hid, g, w, u, gt, tokens):
-    lhs = pl.BlockSpec((1, T, 256), lambda e, c: (e, 0, c))
-    rhs = pl.BlockSpec((1, T, D), lambda e, c: (e, 0, 0))
-    out = pl.BlockSpec((1, 256, D), lambda e, c: (e, c, 0))
-    rows = pl.BlockSpec((64, D), lambda e, c: (e * 4 + c, 0))
+    pairs = [(x_hbm, x), (dpre_hbm, dpre), (hid_hbm, hid), (g_hbm, g)]
+    loads = []
+    for e in range(2):
+        for i, (src, dst) in enumerate(pairs):
+            loads.append(pltpu.make_async_copy(src.at[e], dst.at[e], load.at[e * 4 + i]))
+    rest = [(w_hbm, w), (u_hbm, u), (gt_hbm, gt), (pmt_hbm, pmt), (tok_hbm, tok)]
+    for i, (src, dst) in enumerate(rest):
+        loads.append(pltpu.make_async_copy(src, dst, load.at[8 + i]))
+    for copy in loads:
+        copy.start()
+
+    def outer(e, lhs, rhs, buf, dst, sem):
+        @pl.loop(0, 4)
+        def _(c):
+            rows = pl.ds(pl.multiple_of(c * 256, 256), 256)
+            buf[e, rows, :] = lax.dot_general(
+                lhs[e, :, rows], rhs[e], (((0,), (0,)), ((), ())), preferred_element_type=f32
+            )
+            pltpu.make_async_copy(buf.at[e, rows, :], dst.at[e, rows, :], sem).start()
+
+    for e in range(2):
+        loads[e * 4].wait()
+        loads[e * 4 + 1].wait()
+        outer(e, x, dpre, win, win_out, store.at[0])
+        loads[e * 4 + 2].wait()
+        loads[e * 4 + 3].wait()
+        outer(e, hid, g, wback, wback_out, store.at[1])
+    loads[8].wait()
+    for c, k in ((0, 2), (1, 3), (2, 1)):
+        wqkv[c] = w[:, k * 256 : (k + 1) * 256].astype(f32)
+    for k in range(4):
+        wout[:, k * 256 : (k + 1) * 256] = w[k * 256 : (k + 1) * 256, :256].astype(f32)
+    wq_store = pltpu.make_async_copy(wqkv, wqkv_out, store.at[2])
+    wo_store = pltpu.make_async_copy(wout, wout_out, store.at[3])
+    wq_store.start()
+    wo_store.start()
+    for copy in loads[9:]:
+        copy.wait()
+
+    @pl.loop(0, 2)
+    def _(c):
+        rows = pl.ds(pl.multiple_of(c * 256, 256), 256)
+        out[rows, :] = tok[rows, :].astype(f32) + mm(pmt[rows, :], u[...])
+        pltpu.make_async_copy(out.at[rows, :], out_out.at[rows, :], store.at[4]).start()
+        gtok[rows, :] = mm(pmt[rows, :], gt[...])
+        pltpu.make_async_copy(gtok.at[rows, :], gt_out.at[rows, :], store.at[5]).start()
+
+    pltpu.make_async_copy(win, win_out, store.at[0]).wait()
+    pltpu.make_async_copy(wback, wback_out, store.at[1]).wait()
+    wq_store.wait()
+    wo_store.wait()
+    pltpu.make_async_copy(out, out_out, store.at[4]).wait()
+    pltpu.make_async_copy(gtok, gt_out, store.at[5]).wait()
+
+
+def finish(*operands):
     S = jax.ShapeDtypeStruct
+    hbm = pl.BlockSpec(memory_space=pl.ANY)
+    results = [
+        S((2, D, D), f32), S((2, D, D), f32), S((3, D, 256), f32), S((256, D), f32),
+        S((T, D), f32), S((T, D), f32),
+    ]
+    DMA = pltpu.SemaphoreType.DMA
     return pl.pallas_call(
         finish_kernel,
         name="finish",
-        grid=(2, 4),
-        out_shape=[
-            S((2, D, D), f32), S((2, D, D), f32), S((3, D, 256), f32), S((256, D), f32),
-            S((T, D), f32), S((T, D), f32),
-        ],
-        in_specs=[lhs, rhs, lhs, rhs, pl.BlockSpec((128, D), lambda e, c: (e * 4 + c, 0)),
-                  rows, rows, rows],
-        out_specs=[
-            out, out,
-            pl.BlockSpec((3, 128, 256), lambda e, c: (0, e * 4 + c, 0)),
-            pl.BlockSpec((128, 256), lambda e, c: (c % 2, e * 2 + c // 2)),
-            rows, rows,
-        ],
+        out_shape=results,
+        in_specs=[hbm] * len(operands),
+        out_specs=[hbm] * len(results),
+        scratch_shapes=[pltpu.VMEM(a.shape, a.dtype) for a in (*operands, *results)]
+        + [DMA((13,)), DMA((6,))],
         compiler_params=pltpu.CompilerParams(vmem_limit_bytes=60 << 20),
         cost_estimate=pl.CostEstimate(
             flops=8 * 2**30, bytes_accessed=37 * 2**20, transcendentals=0
         ),
-    )(x, dpre, hid, g, w, u, gt, tokens)
+    )(*operands)
 
 
 def per_device(
@@ -845,12 +940,12 @@
     w_qkv, w_out, w_in, w_back, cotangent,
 ):
     row = lambda v: v.reshape(1, D)
-    x, g, hid, dpre, u, gt, w, nrm = layer(
+    x, g, hid, dpre, u, gt, pmt, w, nrm = layer(
         segment_ids, expert_of.reshape(1, T), row(norm1_gain), row(norm1_bias), row(norm2_gain), row(norm2_bias),
         tokens, w_qkv, w_out, w_in, w_back, cotangent,
     )
     grad_w_in, grad_w_back, grad_w_qkv, grad_w_out, output, grad_tokens = finish(
-        x, dpre, hid, g, w, u, gt, tokens
+        x, dpre, hid, g, w, u, gt, pmt, tokens
     )
     vectors = nrm.reshape(4, D)
     return (

time: 180 us -> 166 us (0.922)
  Pallas kernels: 178 us -> 164 us
    pallas_call x1, Pallas kernels: 162 us -> 151 us  [layer(): pl.pallas_call(layer_kernel, name='layer', out_shape=[quarters] * 4 + [S(...]
    pallas_call x1, Pallas kernels: 16 us -> 12.8 us  [finish(): pl.pallas_call(finish_kernel, name='finish', out_shape=results, in_specs=...]
where the time goes in v3:
time: 166 us
  Pallas kernels  164 us (99%)
    pallas_call x1, Pallas kernels, layer(): pl.pallas_call(layer_kernel, name='layer', out_shape=[quarters] * 4 + [S(...  151 us
    pallas_call x1, Pallas kernels, finish(): pl.pallas_call(finish_kernel, name='finish', out_shape=results, in_specs=...  12.8 us

profile of v3, /device:TPU:1, one launch (start us, length us, event | category | flops | bytes accessed | tf_op | source)
XLA Modules:
  0.0 165.6 jit_solution(14745733392829382233)
XLA Ops:
  0.6 150.7 %layer.1 = (bf16[2,512,1024]{2,1,0:T(8,128)(2,1)}, bf16[2,512,1024]{2,1,0:T(8,128)(2,1)}, bf16[2,512,1024]{2,1,0:T(8,128)(2,1)}, bf16[2,512,1024]{2,1,0:T(8,128)...) custom-call(s32[1,512]{1,0:T(1,128)} %seg_ref.1, ...), custom_call_target="tpu_custom_call" | custom-call | flops 24000000000 | bytes 31457280 | tf_op jit(solution)/shard_map/layer/pallas_call | solution.py:838
  151.4 1.3 slice_bitcast_fusion
  152.7 12.8 %finish.1 = (f32[2,1024,1024]{2,1,0:T(8,128)}, f32[2,1024,1024]{2,1,0:T(8,128)}, f32[3,1024,256]{2,1,0:T(8,128)}, f32[256,1024]{1,0:T(8,128)}, f32[512,1024]{1,0:T(8,128)}, /*index=5*/f32[512,1024]{1,0:T(8,128)}) custom-call(bf16[2,512,1024]{2,1,0:T(8,128)(2,1)} %get-tuple-element.25.x_hbm, bf16[2,512,1024]{2,1,0:T(8,128)(2,1)} %get-tuple-element.26.dpre_hbm, ...), custom_call_target="tpu_custom_call" | custom-call | flops 8589934592 | bytes 38797312 | tf_op jit(solution)/shard_map/finish/pallas_call | solution.py:923

commit v4 on v3

--- a/solution.py
+++ b/solution.py
@@ -212,8 +212,7 @@
     datt, dmx, v_t, dqkv,
     d_rel, d_sum, d_arr, gtall,
     wx, wfin,
-    w0, w0_rel, w0_sum, w0_arr, w1, w1_rel, w1_sum, w1_arr,
-    w2_rel, w2_sum, w2_arr, w3_rel, w3_sum, w3_arr,
+    wbox,
     nv, nrx, nye,
     loc, cs, ns, es, os_, rss, ags, xs, vs,
 ):
@@ -221,15 +220,8 @@
     h = lax.axis_index("head")
     core = lax.rem(me, 2)
     chip = me // 2
-    y = lax.rem(chip, 4)
-    z = chip // 4
-
-    def at_yz(yy, zz, cc):
-        return {"expert": (rem4(zz) * 4 + rem4(yy)) * 2 + cc}
 
     ring_x = (h, {"head": rem4(h + 1)}, {"head": rem4(h + 3)})
-    ring_y = (y, at_yz(y + 1, z, core), at_yz(y + 3, z, core))
-    ring_z = (z, at_yz(y, z + 1, core), at_yz(y, z + 3, core))
     sibling = {"expert": chip * 2 + 1 - core}
     left, right, far = rem4(h + 3), rem4(h + 1), rem4(h + 2)
 
@@ -576,46 +568,33 @@
 
     class WeightSum:
         def __init__(self, k):
-            cols, thin = pl.ds(k * T, T), pl.ds(k * 256, 256)
-            both = pl.ds(0, 2)
+            cols, self.sem = pl.ds(k * T, T), xs.at[k]
             core_rows = pl.ds(pl.multiple_of(core * T, T), T)
             other_rows = pl.ds(pl.multiple_of((1 - core) * T, T), T)
-            base = core * T
             self.mine, self.got, self.ws = wpart.at[core, :, cols], wx.at[:, cols], ws.at[:, cols]
-            self.w0, self.w1 = w0.at[:, cols], w1.at[:, cols]
-            sem = xs.at[k]
-            self.swap = remote(
-                wpart.at[1 - core, :, cols], self.got, sem.at[0], sem.at[1], sibling
-            )
-
-            def scatter(ring, part, rows, bufs, at):
-                rel, tot, arr = bufs
-                return ReduceScatter(
-                    ring, part, rows, rel.at[both, :, thin], tot.at[both, :, thin],
-                    arr.at[both, both, :, thin], rss.at[6 + 4 * k + at],
-                )
-
-            def spread(ring, row0, rows, at):
-                view = wfin.at[pl.ds(pl.multiple_of(row0, rows), 4 * rows), cols]
-                return Gather(ring, view, rows, ags.at[5 + 4 * k + at])
-
-            self.rs0 = scatter(ring_y, ws.at[pl.ds(0, 256), cols], 64, (w0_rel, w0_sum, w0_arr), 0)
-            self.rs1 = scatter(ring_z, ws.at[pl.ds(256, 256), cols], 64, (w1_rel, w1_sum, w1_arr), 1)
-            self.rs2 = scatter(ring_z, self.w0, 16, (w2_rel, w2_sum, w2_arr), 2)
-            self.rs3 = scatter(ring_y, self.w1, 16, (w3_rel, w3_sum, w3_arr), 3)
-            row_y, row_z = base + y * 64, base + 256 + z * 64
-            self.last = [
-                wfin.at[pl.ds(pl.multiple_of(row_y + z * 16, 16), 16), cols],
-                wfin.at[pl.ds(pl.multiple_of(row_z + y * 16, 16), 16), cols],
-            ]
-            self.ag0, self.ag1 = spread(ring_y, base, 64, 0), spread(ring_z, base + 256, 64, 1)
-            self.ag2, self.ag3 = spread(ring_z, row_y, 16, 2), spread(ring_y, row_z, 16, 3)
-            done = wfin.at[core_rows, cols]
-            self.give = remote(done, done, sem.at[2], sem.at[3], sibling)
-            self.take = remote(done, wfin.at[other_rows, cols], sem.at[2], sem.at[3], sibling)
+            self.box, self.full = wbox.at[:, cols], wfin.at[core_rows, cols]
+            self.swap = self.copy(wpart.at[1 - core, :, cols], self.got, 0, sibling)
+            first = pl.ds(0, 15 * 32)
+            self.boxes = self.copy(self.ws.at[first, :], self.box.at[first, :], 2, sibling)
+            self.rest = self.copy(self.full.at[first, :], self.full.at[first, :], 4, sibling)
+            self.give = self.copy(self.full, self.full, 6, sibling)
+            self.take = self.copy(self.full, wfin.at[other_rows, cols], 6, sibling)
             self.store = pltpu.make_async_copy(
                 wfin.at[:, cols], w_out.at[:, cols], loc.at[12 + k]
             )
+
+        def copy(self, src, dst, at, device):
+            return remote(src, dst, self.sem.at[at], self.sem.at[at + 1], device)
+
+        def block(self, ref, c):
+            return ref.at[pl.ds(pl.multiple_of(c * 32, 32), 32), :]
+
+        def to_chips(self, src, dst, at):
+            @pl.loop(1, 16)
+            def _(k):
+                c = lax.rem(chip + k, 16)
+                block = self.block(src, chip if src is dst else c)
+                self.copy(block, self.block(dst, chip), at, {"expert": c * 2 + core}).start()
 
         def step(self, n):
             if n == 0:
@@ -623,53 +602,25 @@
             elif n == 1:
                 self.swap.wait_recv()
                 self.ws[...] = (self.mine[...].astype(f32) + self.got[...].astype(f32)).astype(bf16)
-                self.rs0.send_all()
-                self.rs1.send_all()
+                self.to_chips(self.ws, self.box, 2)
+                self.block(self.box, chip)[...] = self.block(self.ws, chip)[...]
             elif n == 2:
-                self.rs0.pass_on()
-                self.rs1.pass_on()
+                self.boxes.wait_recv()
+                total = self.box[0:32, :].astype(f32)
+                for c in range(1, 16):
+                    total += self.box[c * 32 : c * 32 + 32, :].astype(f32)
+                self.block(self.full, chip)[...] = total.astype(bf16)
+                self.to_chips(self.full, self.full, 4)
             elif n == 3:
-                self.rs0.wait()
-                self.w0[...] = self.rs0.value().astype(bf16)
-                self.rs2.send_all()
-                self.rs1.wait()
-                self.w1[...] = self.rs1.value().astype(bf16)
-                self.rs3.send_all()
-            elif n == 4:
-                self.rs2.pass_on()
-                self.rs3.pass_on()
-            elif n == 5:
-                self.rs2.wait()
-                self.last[0][...] = self.rs2.value().astype(bf16)
-                self.ag2.start()
-                self.rs3.wait()
-                self.last[1][...] = self.rs3.value().astype(bf16)
-                self.ag3.start()
-            elif n == 6:
-                self.ag2.pass_on()
-                self.ag3.pass_on()
-            elif n == 7:
-                self.ag2.wait_rest()
-                self.ag0.start()
-                self.ag3.wait_rest()
-                self.ag1.start()
-            elif n == 8:
-                self.ag0.pass_on()
-                self.ag1.pass_on()
-            elif n == 9:
-                self.ag0.wait_rest()
-                self.ag1.wait_rest()
+                self.rest.wait_recv()
                 self.give.start()
             else:
                 self.take.wait_recv()
                 self.store.start()
 
         def wait_sent(self):
-            self.swap.wait_send()
-            self.give.wait_send()
-            for group in (self.rs0, self.rs1, self.rs2, self.rs3,
-                          self.ag0, self.ag1, self.ag2, self.ag3):
-                group.wait_sent()
+            for copy in (self.swap, self.boxes, self.rest, self.give):
+                copy.wait_send()
             self.store.wait()
 
     sum_a = WeightSum(0)
@@ -692,14 +643,12 @@
     sum_a.step(1)
     rs_o[1].pass_on()
     pl.loop(2, 4)(backward)
-    sum_a.step(2)
     rs_o[0].wait()
     send_back(rs_o[0], 0, osend, o_x)
     for hp in range(2):
         pair = slice(hp * 128, hp * 128 + 128)
         dks = [mm(dss[hd][...], qkv[0, :, head(hd)]) for hd in (2 * hp, 2 * hp + 1)]
         dqkv[1, :, pair] = jnp.concatenate(dks, axis=1).astype(bf16)
-    sum_a.step(3)
 
     rs_d = ReduceScatter(ring_x, npart, Q, d_rel, d_sum, d_arr, rss.at[5])
 
@@ -723,13 +672,11 @@
     weight_part(1, slice(768, 1024))
     sum_b = WeightSum(1)
     sum_b.step(0)
-    sum_a.step(4)
+    sum_a.step(2)
     rs_d.pass_on()
-    sum_a.step(5)
+    sum_b.step(1)
     rs_o[1].wait()
     send_back(rs_o[1], 1, osend, o_x)
-    sum_b.step(1)
-    sum_a.step(6)
 
     xhat1, r1 = norm_parts(xp[own_rows, :].astype(f32))
     rs_d.wait()
@@ -751,9 +698,8 @@
         return remote(three, three, vs.at[at], vs.at[at + 1], {"head": rem4(h + 1)})
 
     nx = to_x(lambda k: nv.at[k], nrx, h, 0)
+    sum_a.step(3)
     sum_b.step(2)
-    sum_a.step(7)
-    sum_b.step(3)
     nx.wait_recv()
     nye[me] = nv[h] + nrx[rem4(h + 1)] + nrx[rem4(h + 2)] + nrx[rem4(h + 3)]
 
@@ -763,34 +709,27 @@
     n_rows = nye.at[pl.ds(0, G - 1)]
     n_every = remote(n_rows, n_rows, vs.at[2], vs.at[3], {"expert": lax.rem(me + 1, G)})
     others(lambda d: n_all(d).start())
-    sum_a.step(8)
     ag_g.pass_on()
-    sum_b.step(4)
 
     for e in range(2):
         o_x[e].all.wait_recv()
     outall[own_rows, :] = (att_q[...] + to_tokens(orecv, 0) + to_tokens(orecv, 1)).astype(bf16)
     ag_o = Gather(ring_x, outall, Q, ags.at[4])
     ag_o.start()
-    sum_b.step(5)
-    sum_a.step(9)
-    sum_b.step(6)
+    sum_a.step(4)
     n_every.wait_recv()
     nrm_out[h] = jnp.sum(nye[...], axis=0)
     nf = to_x(lambda k: nrm_out.at[h], nrm_out, h, 4)
-    sum_b.step(7)
-    sum_a.step(10)
+    sum_b.step(3)
     ag_o.pass_on()
-    sum_b.step(8)
     ag_g.wait_rest()
     gt_store = pltpu.make_async_copy(gtall, gt_out, loc.at[14])
     gt_store.start()
-    sum_b.step(9)
+    nf.wait_recv()
+    sum_b.step(4)
     ag_o.wait_rest()
     u_store = pltpu.make_async_copy(outall, u_out, loc.at[11])
     u_store.start()
-    nf.wait_recv()
-    sum_b.step(10)
 
     for x in n_x + e_x + o_x:
         x.all.wait_send()
@@ -828,10 +767,9 @@
         V((T, D), bf16), V((T, 256), bf16), V((256, T), bf16), V((3, T, 256), bf16),
         *rs_bufs(Q, HALF), V((T, D), bf16),
         V((T, D), bf16), V((D, D), bf16),
-        V((64, D), bf16), *rs_bufs(64, HALF), V((64, D), bf16), *rs_bufs(64, HALF),
-        *rs_bufs(16, HALF), *rs_bufs(16, HALF),
+        V((T, D), bf16),
         V((4, 8, 128), f32), V((4, 8, 128), f32), V((G, 8, 128), f32),
-        DMA((15,)), *[DMA((2, 2))] * 4, DMA((14, 4)), DMA((13, 4)), DMA((2, 4)), DMA((6,)),
+        DMA((15,)), *[DMA((2, 2))] * 4, DMA((6, 4)), DMA((5, 4)), DMA((2, 8)), DMA((6,)),
     ]
     S = jax.ShapeDtypeStruct
     quarters = S((2, T, D), bf16)
@@ -853,10 +791,12 @@
 
 
 def finish_kernel(
-    x_hbm, dpre_hbm, hid_hbm, g_hbm, w_hbm, u_hbm, gt_hbm, pmt_hbm, tok_hbm,
-    win_out, wback_out, wqkv_out, wout_out, out_out, gt_out,
+    x_hbm, dpre_hbm, hid_hbm, g_hbm, w_hbm, u_hbm, gt_hbm, pmt_hbm, tok_hbm, nrm,
+    win_out, wback_out, wqkv_out, wout_out, out_out, gt_out, n0, n1, n2, n3,
     x, dpre, hid, g, w, u, gt, pmt, tok, win, wback, wqkv, wout, out, gtok, load, store,
 ):
+    for k, vector in enumerate((n0, n1, n2, n3)):
+        vector[...] = nrm[k]
     pairs = [(x_hbm, x), (dpre_hbm, dpre), (hid_hbm, hid), (g_hbm, g)]
     loads = []
     for e in range(2):
@@ -912,9 +852,10 @@
     pltpu.make_async_copy(gtok, gt_out, store.at[5]).wait()
 
 
-def finish(*operands):
+def finish(nrm, *operands):
     S = jax.ShapeDtypeStruct
     hbm = pl.BlockSpec(memory_space=pl.ANY)
+    vmem = pl.BlockSpec(memory_space=pltpu.VMEM)
     results = [
         S((2, D, D), f32), S((2, D, D), f32), S((3, D, 256), f32), S((256, D), f32),
         S((T, D), f32), S((T, D), f32),
@@ -923,16 +864,16 @@
     return pl.pallas_call(
         finish_kernel,
         name="finish",
-        out_shape=results,
-        in_specs=[hbm] * len(operands),
-        out_specs=[hbm] * len(results),
+        out_shape=results + [S((8, 128), f32)] * 4,
+        in_specs=[hbm] * len(operands) + [vmem],
+        out_specs=[hbm] * len(results) + [vmem] * 4,
         scratch_shapes=[pltpu.VMEM(a.shape, a.dtype) for a in (*operands, *results)]
         + [DMA((13,)), DMA((6,))],
         compiler_params=pltpu.CompilerParams(vmem_limit_bytes=60 << 20),
         cost_estimate=pl.CostEstimate(
             flops=8 * 2**30, bytes_accessed=37 * 2**20, transcendentals=0
         ),
-    )(*operands)
+    )(*operands, nrm)
 
 
 def per_device(
@@ -944,10 +885,10 @@
         segment_ids, expert_of.reshape(1, T), row(norm1_gain), row(norm1_bias), row(norm2_gain), row(norm2_bias),
         tokens, w_qkv, w_out, w_in, w_back, cotangent,
     )
-    grad_w_in, grad_w_back, grad_w_qkv, grad_w_out, output, grad_tokens = finish(
-        x, dpre, hid, g, w, u, gt, pmt, tokens
+    grad_w_in, grad_w_back, grad_w_qkv, grad_w_out, output, grad_tokens, *vectors = finish(
+        nrm, x, dpre, hid, g, w, u, gt, pmt, tokens
     )
-    vectors = nrm.reshape(4, D)
+    vectors = [v.reshape(D) for v in vectors]
     return (
         output, grad_tokens, vectors[0], vectors[1], vectors[2], vectors[3],
         grad_w_qkv, grad_w_out, grad_w_in, grad_w_back,

time: 166 us -> 157 us (0.946)
  Pallas kernels: 164 us -> 156 us
    pallas_call x1, Pallas kernels: 151 us -> 142 us  [layer(): pl.pallas_call(layer_kernel, name='layer', out_shape=[quarters] * 4 + [S(...]
where the time goes in v4:
time: 157 us
  Pallas kernels  156 us (99%)
    pallas_call x1, Pallas kernels, layer(): pl.pallas_call(layer_kernel, name='layer', out_shape=[quarters] * 4 + [S(...  142 us
    pallas_call x1, Pallas kernels, finish(): pl.pallas_call(finish_kernel, name='finish', out_shape=results + [S((8, 1...  14.1 us

profile of v4, /device:TPU:1, one launch (start us, length us, event | category | flops | bytes accessed | tf_op | source)
XLA Modules:
  0.0 157.1 jit_solution(1992490545515078403)
XLA Ops:
  0.6 142.2 %layer.1 = (bf16[2,512,1024]{2,1,0:T(8,128)(2,1)}, bf16[2,512,1024]{2,1,0:T(8,128)(2,1)}, bf16[2,512,1024]{2,1,0:T(8,128)(2,1)}, bf16[2,512,1024]{2,1,0:T(8,128)...) custom-call(s32[1,512]{1,0:T(1,128)} %seg_ref.1, ...), custom_call_target="tpu_custom_call" | custom-call | flops 24000000000 | bytes 31457280 | tf_op jit(solution)/shard_map/layer/pallas_call | solution.py:776
  142.8 14.1 %finish.1 = (f32[2,1024,1024]{2,1,0:T(8,128)}, f32[2,1024,1024]{2,1,0:T(8,128)}, f32[3,1024,256]{2,1,0:T(8,128)}, f32[256,1024]{1,0:T(8,128)}, f32[512,1024]{1,0...) custom-call(bf16[2,512,1024]{2,1,0:T(8,128)(2,1)} %get-tuple-element, ...), custom_call_target="tpu_custom_call" | custom-call | flops 8589934592 | bytes 38797312 | tf_op jit(solution)/shard_map/finish/pallas_call | solution.py:864

commit v5 on v4

--- a/solution.py
+++ b/solution.py
@@ -453,13 +453,11 @@
     loads["win"].wait()
     loads["wbk"].wait()
 
-    def unit(e):
-        @pl.loop(0, 2)
-        def _(c):
-            cols = pl.ds(pl.multiple_of(c * 512, 512), 512)
-            act, slope = gelu_parts(mm(xall[e], win[e, :, cols]))
-            hid[e, :, cols] = act.astype(bf16)
-            dpre[e, :, cols] = (mm_nt(gal[e], wbk[e, cols, :]) * slope).astype(bf16)
+    def unit(e, c):
+        cols = pl.ds(c * 512, 512)
+        act, slope = gelu_parts(mm(xall[e], win[e, :, cols]))
+        hid[e, :, cols] = act.astype(bf16)
+        dpre[e, :, cols] = (mm_nt(gal[e], wbk[e, cols, :]) * slope).astype(bf16)
 
     def unit_n2(e):
         @pl.loop(0, 2)
@@ -483,8 +481,9 @@
     rs_o = [scatter(outp, (o_rel, o_sum, o_arr), e, 3 + e) for e in range(2)]
 
     ag_x[0].wait_rest()
-    unit(0)
+    unit(0, 0)
     ag_x[1].pass_on()
+    unit(0, 1)
     unit_n2(0)
     rs_e[0].send_all()
     for x in cot_x:
@@ -492,8 +491,9 @@
     unit_out(0)
     regroup(1)
     ag_x[1].wait_rest()
-    unit(1)
+    unit(1, 0)
     rs_e[0].pass_on()
+    unit(1, 1)
     unit_n2(1)
     rs_e[1].send_all()
     unit_out(1)
@@ -795,8 +795,10 @@
     win_out, wback_out, wqkv_out, wout_out, out_out, gt_out, n0, n1, n2, n3,
     x, dpre, hid, g, w, u, gt, pmt, tok, win, wback, wqkv, wout, out, gtok, load, store,
 ):
-    for k, vector in enumerate((n0, n1, n2, n3)):
-        vector[...] = nrm[k]
+    vectors = [
+        pltpu.make_async_copy(nrm.at[k], vector, store.at[6 + k])
+        for k, vector in enumerate((n0, n1, n2, n3))
+    ]
     pairs = [(x_hbm, x), (dpre_hbm, dpre), (hid_hbm, hid), (g_hbm, g)]
     loads = []
     for e in range(2):
@@ -805,7 +807,7 @@
     rest = [(w_hbm, w), (u_hbm, u), (gt_hbm, gt), (pmt_hbm, pmt), (tok_hbm, tok)]
     for i, (src, dst) in enumerate(rest):
         loads.append(pltpu.make_async_copy(src, dst, load.at[8 + i]))
-    for copy in loads:
+    for copy in loads + vectors:
         copy.start()
 
     def outer(e, lhs, rhs, buf, dst, sem):
@@ -850,12 +852,13 @@
     wo_store.wait()
     pltpu.make_async_copy(out, out_out, store.at[4]).wait()
     pltpu.make_async_copy(gtok, gt_out, store.at[5]).wait()
+    for copy in vectors:
+        copy.wait()
 
 
 def finish(nrm, *operands):
     S = jax.ShapeDtypeStruct
     hbm = pl.BlockSpec(memory_space=pl.ANY)
-    vmem = pl.BlockSpec(memory_space=pltpu.VMEM)
     results = [
         S((2, D, D), f32), S((2, D, D), f32), S((3, D, 256), f32), S((256, D), f32),
         S((T, D), f32), S((T, D), f32),
@@ -865,10 +868,10 @@
         finish_kernel,
         name="finish",
         out_shape=results + [S((8, 128), f32)] * 4,
-        in_specs=[hbm] * len(operands) + [vmem],
-        out_specs=[hbm] * len(results) + [vmem] * 4,
+        in_specs=[hbm] * (len(operands) + 1),
+        out_specs=[hbm] * (len(results) + 4),
         scratch_shapes=[pltpu.VMEM(a.shape, a.dtype) for a in (*operands, *results)]
-        + [DMA((13,)), DMA((6,))],
+        + [DMA((13,)), DMA((10,))],
         compiler_params=pltpu.CompilerParams(vmem_limit_bytes=60 << 20),
         cost_estimate=pl.CostEstimate(
             flops=8 * 2**30, bytes_accessed=37 * 2**20, transcendentals=0

time: 157 us -> 156 us (level)
  no operation moved by 1% of the time
where the time goes in v5:
time: 156 us
  Pallas kernels  155 us (99%)
    pallas_call x1, Pallas kernels, layer(): pl.pallas_call(layer_kernel, name='layer', out_shape=[quarters] * 4 + [S(...  142 us
    pallas_call x1, Pallas kernels, finish(): pl.pallas_call(finish_kernel, name='finish', out_shape=results + [S((8, 1...  12.9 us

profile of v5, /device:TPU:1, one launch (start us, length us, event | category | flops | bytes accessed | tf_op | source)
XLA Modules:
  0.0 155.8 jit_solution(5373841117147131401)
XLA Ops:
  0.6 142.1 %layer.1 = (bf16[2,512,1024]{2,1,0:T(8,128)(2,1)}, bf16[2,512,1024]{2,1,0:T(8,128)(2,1)}, bf16[2,512,1024]{2,1,0:T(8,128)(2,1)}, bf16[2,512,1024]{2,1,0:T(8,128)...) custom-call(s32[1,512]{1,0:T(1,128)} %seg_ref.1, ...), custom_call_target="tpu_custom_call" | custom-call | flops 24000000000 | bytes 31457280 | tf_op jit(solution)/shard_map/layer/pallas_call | solution.py:776
  142.8 12.9 %finish.1 = (f32[2,1024,1024]{2,1,0:T(8,128)}, f32[2,1024,1024]{2,1,0:T(8,128)}, f32[3,1024,256]{2,1,0:T(8,128)}, f32[256,1024]{1,0:T(8,128)}, f32[512,1024]{1,0...) custom-call(bf16[2,512,1024]{2,1,0:T(8,128)(2,1)} %get-tuple-element, ...), custom_call_target="tpu_custom_call" | custom-call | flops 8589934592 | bytes 38797312 | tf_op jit(solution)/shard_map/finish/pallas_call | solution.py:867

commit v6 on v5

--- a/solution.py
+++ b/solution.py
@@ -528,13 +528,12 @@
     rs_e[0].wait()
     send_back(rs_e[0], 0, esend, e_x)
     rs_e[1].pass_on()
+    rs_e[1].wait()
     rs_o[0].send_all()
-    rs_e[1].wait()
     send_back(rs_e[1], 1, esend, e_x)
 
     e_x[0].all.wait_recv()
     dn2 = to_tokens(erecv, 0)
-    rs_o[0].pass_on()
     e_x[1].all.wait_recv()
     dn2 = dn2 + to_tokens(erecv, 1)
     xhat2, r2 = resid_norm()
@@ -546,6 +545,7 @@
     ag_d = Gather(ring_x, datt, Q, ags.at[2])
     ag_d.start()
     ag_d.pass_on()
+    rs_o[0].pass_on()
     rs_o[1].send_all()
     ag_d.wait_rest()
 

time: 156 us -> 154 us (0.987)
  no operation moved by 1% of the time
where the time goes in v6:
time: 154 us
  Pallas kernels  154 us (100%)
    pallas_call x1, Pallas kernels, layer(): pl.pallas_call(layer_kernel, name='layer', out_shape=[quarters] * 4 + [S(...  141 us
    pallas_call x1, Pallas kernels, finish(): pl.pallas_call(finish_kernel, name='finish', out_shape=results + [S((8, 1...  12.9 us

profile of v6, /device:TPU:1, one launch (start us, length us, event | category | flops | bytes accessed | tf_op | source)
XLA Modules:
  0.0 154.3 jit_solution(7885613474312859486)
XLA Ops:
  0.6 140.6 %layer.1 = (bf16[2,512,1024]{2,1,0:T(8,128)(2,1)}, bf16[2,512,1024]{2,1,0:T(8,128)(2,1)}, bf16[2,512,1024]{2,1,0:T(8,128)(2,1)}, bf16[2,512,1024]{2,1,0:T(8,128)...) custom-call(s32[1,512]{1,0:T(1,128)} %seg_ref.1, ...), custom_call_target="tpu_custom_call" | custom-call | flops 24000000000 | bytes 31457280 | tf_op jit(solution)/shard_map/layer/pallas_call | solution.py:776
  141.3 12.9 %finish.1 = (f32[2,1024,1024]{2,1,0:T(8,128)}, f32[2,1024,1024]{2,1,0:T(8,128)}, f32[3,1024,256]{2,1,0:T(8,128)}, f32[256,1024]{1,0:T(8,128)}, f32[512,1024]{1,0...) custom-call(bf16[2,512,1024]{2,1,0:T(8,128)(2,1)} %get-tuple-element, ...), custom_call_target="tpu_custom_call" | custom-call | flops 8589934592 | bytes 38797312 | tf_op jit(solution)/shard_map/finish/pallas_call | solution.py:867
